TPU v7x, 128 devices: a whole 4x4x4 slice. The times are simulated.
128 devices in a mesh: row: 8 (over x_hi, y), diag: 16 (over z, x_lo, core).
Axes of the slice: x: 4 (x_hi: 2, x_lo: 2; x = x_hi * 2 + x_lo), y: 4, z: 4, core: 2. Of those that a mesh axis runs over, the one named last changes fastest.
Arguments:
- bins_x: bfloat16 [8192, 256], P(('row', 'diag')), may hold values from -6 to 6
- proj_weight: bfloat16 [256, 64], replicated, may hold values from -0.375 to 0.375
- convolution_weight: bfloat16 [9, 32, 32], replicated, may hold values from -0.375 to 0.375
- convolution_bias: float32 [32], replicated, may hold values from -4 to 4
- readout: float32 [32], replicated, may hold values from -1 to 1
- targets: bfloat16 [64, 128, 2048], P('row', None, 'diag'), may hold values from -6 to 6
- block_order: int32 [64], replicated, may hold values from 0 to 63, each once
- band_reach: int32 [64], replicated, may hold values from 512 to 1919
Outputs:
- codes_grad: float32 [8192, 64], P(('row', 'diag'))
- conv_grad: float32 [9216], P(('row', 'diag'))
All inputs are finite; a program needn't handle non-finite values.
Results may differ from a plain program's by a relative error of at most 0.0016.
Values may be sent and summed in bfloat16 or wider, within the bound.
No kernel may reach another device: no remote copies, remote signals or barrier semaphores. Data moves between devices by JAX's collectives and lax.ppermute only.
A program may use at most 256 MiB of HBM per device.

v0:
```python
import jax
import jax.numpy as jnp
from jax import lax
from jax.sharding import PartitionSpec as P

C = 32
TILE_SIDE_BINS = 128
DILATION_STEP = 16
BAND_TILE_COUNT = 16


SQRT_HALF = 0.7071067811865476
INV_SQRT_TAU = 0.3989422804014327


def with_halo(value, sides, width):
    for axis, dim in sides:
        peers, length = (lax.axis_size(axis), value.shape[dim])
        up = [(i, (i + 1) % peers) for i in range(peers - 1)]
        down = [(j, i) for i, j in up]
        last = lax.slice_in_dim(value, length - width, length, axis=dim)
        leading = lax.slice_in_dim(value, 0, width, axis=dim)
        before = lax.ppermute(last, axis, up)
        after = lax.ppermute(leading, axis, down)
        value = jnp.concatenate([before, value, after], axis=dim)
    return value


def grid_cells(row_cell_ids, column_cell_ids, block_total):
    row_blocks = jnp.floor_divide(row_cell_ids, TILE_SIDE_BINS)[:, None]
    col_blocks = jnp.floor_divide(column_cell_ids, TILE_SIDE_BINS)[None, :]
    return (
        (row_blocks >= 0)
        & (row_blocks < block_total)
        & (col_blocks >= row_blocks)
        & (col_blocks - row_blocks < BAND_TILE_COUNT)
        & (col_blocks < block_total)
    )


def loss_cells(row_cell_ids, column_cell_ids, band_reach, block_total):
    in_grid = grid_cells(row_cell_ids, column_cell_ids, block_total)
    row_blocks = jnp.floor_divide(row_cell_ids, TILE_SIDE_BINS)
    labels = jnp.arange(block_total, dtype=jnp.int32)
    reach_rows = jnp.sum(
        jnp.where(row_blocks[:, None] == labels[None, :], band_reach[None, :], 0), axis=1
    )
    distance = column_cell_ids[None, :] - row_cell_ids[:, None]
    return in_grid & (distance >= 0) & (distance <= reach_rows[:, None])


def build_pair_maps(
    padded_codes, row_begin, column_begin, output_rows, output_columns, border_width, block_total
):
    row_code_values = lax.dynamic_slice_in_dim(
        padded_codes,
        row_begin - border_width + 2 * DILATION_STEP,
        output_rows + 2 * border_width,
        0,
    ).astype(jnp.float32)
    column_codes = lax.dynamic_slice_in_dim(
        padded_codes,
        column_begin - border_width + 2 * DILATION_STEP,
        output_columns + 2 * border_width,
        0,
    ).astype(jnp.float32)
    row_cell_ids = (
        row_begin - border_width + jnp.arange(output_rows + 2 * border_width, dtype=jnp.int32)
    )
    column_cell_ids = (
        column_begin - border_width + jnp.arange(output_columns + 2 * border_width, dtype=jnp.int32)
    )
    u_rows = row_code_values[:, :C].T
    w_rows = row_code_values[:, C:].T
    u_cols = column_codes[:, :C].T
    w_cols = column_codes[:, C:].T
    pairwise_maps = (
        u_rows[:, :, None] + u_cols[:, None, :] + w_rows[:, :, None] * w_cols[:, None, :]
    )
    in_grid = grid_cells(row_cell_ids, column_cell_ids, block_total)
    return jnp.where(in_grid[None], pairwise_maps, 0.0).astype(jnp.bfloat16)


def convolution_forward(pairwise_maps, weights, convolution_bias, output_rows, output_columns):
    summed = jnp.zeros((C, output_rows, output_columns), jnp.float32)
    for tap_index in range(9):
        kernel_tap_row = tap_index // 3
        kernel_tap_column = tap_index % 3
        displaced_maps = pairwise_maps[
            :,
            DILATION_STEP * kernel_tap_row : DILATION_STEP * kernel_tap_row + output_rows,
            DILATION_STEP * kernel_tap_column : DILATION_STEP * kernel_tap_column + output_columns,
        ]
        summed = summed + jnp.einsum(
            "oc,cpq->opq", weights[tap_index], displaced_maps, preferred_element_type=jnp.float32
        )
    return summed + convolution_bias[:, None, None]


def conv_transpose(grad_maps, weights, output_rows, output_columns):
    summed = jnp.zeros((C, output_rows, output_columns), jnp.float32)
    for tap_index in range(9):
        kernel_tap_row = tap_index // 3
        kernel_tap_column = tap_index % 3
        displaced_maps = grad_maps[
            :,
            DILATION_STEP * (2 - kernel_tap_row) : DILATION_STEP * (2 - kernel_tap_row)
            + output_rows,
            DILATION_STEP * (2 - kernel_tap_column) : DILATION_STEP * (2 - kernel_tap_column)
            + output_columns,
        ]
        summed = summed + jnp.einsum(
            "oc,opq->cpq", weights[tap_index], displaced_maps, preferred_element_type=jnp.float32
        )
    return summed


def head_grads(convolution_output, target, mask, readout):
    normal_cdf = 0.5 * (1.0 + jax.scipy.special.erf(convolution_output * SQRT_HALF))
    density = jnp.exp(-0.5 * convolution_output * convolution_output) * INV_SQRT_TAU
    pred = jnp.sum(readout[:, None, None] * convolution_output * normal_cdf, axis=0)
    mismatch = jnp.where(mask, pred - target, 0.0) * TILE_SIDE_BINS ** (-0.5)
    return (
        readout[:, None, None] * mismatch[None] * (normal_cdf + convolution_output * density)
    ).astype(jnp.bfloat16)


def extend_rims(receptive_maps):
    spanned_columns = receptive_maps.shape[3]
    broadened_maps = with_halo(receptive_maps, (("diag", 3),), DILATION_STEP)
    trailing_edges = broadened_maps[:, :, TILE_SIDE_BINS - DILATION_STEP :, :]
    leading_edges = broadened_maps[:, :, :DILATION_STEP, :]
    packed = jnp.stack([trailing_edges, leading_edges], axis=1)
    adjacent_tiles = with_halo(packed, (("diag", 1),), 1)
    below_source = jnp.concatenate(
        [adjacent_tiles[:, 0, :, :, :spanned_columns], leading_edges], axis=3
    )[
        :,
        :,
        :,
        spanned_columns - TILE_SIDE_BINS : 2 * spanned_columns - TILE_SIDE_BINS + 2 * DILATION_STEP,
    ]
    upper_source_rows = jnp.concatenate(
        [trailing_edges, adjacent_tiles[:, 3, :, :, 2 * DILATION_STEP :]], axis=3
    )[:, :, :, TILE_SIDE_BINS : TILE_SIDE_BINS + spanned_columns + 2 * DILATION_STEP]
    paired = jnp.stack([upper_source_rows, below_source], axis=1)
    stacked = with_halo(paired, (("row", 0),), 1)
    return jnp.concatenate([stacked[:-2, 0], broadened_maps, stacked[2:, 1]], axis=2)


def per_device(
    bins_x,
    proj_weight,
    convolution_weight,
    convolution_bias,
    readout,
    targets,
    block_order,
    band_reach,
):
    row_count = targets.shape[0]
    spanned_columns = targets.shape[2]
    block_total = block_order.shape[0]
    bins_total = block_total * TILE_SIDE_BINS
    row_id = lax.axis_index("row")
    diag_id = lax.axis_index("diag")
    code_local = jnp.dot(bins_x, proj_weight, preferred_element_type=jnp.float32).astype(
        jnp.bfloat16
    )
    code_rows = lax.all_gather(code_local, ("row", "diag"), axis=0, tiled=True)
    positions = jnp.arange(block_total, dtype=jnp.int32)
    inverse = jnp.sum(
        jnp.where(block_order[:, None] == positions[None, :], positions[:, None], 0), axis=0
    )
    binned_codes = jnp.take(
        code_rows.reshape(block_total, TILE_SIDE_BINS, 2 * C), inverse, axis=0
    ).reshape(bins_total, 2 * C)
    padded_codes = jnp.pad(
        binned_codes,
        ((2 * DILATION_STEP, BAND_TILE_COUNT * TILE_SIDE_BINS + 2 * DILATION_STEP), (0, 0)),
    )
    block_ids = jnp.arange(row_count, dtype=jnp.int32)

    def anchor(block_index):
        row_begin = (row_id * row_count + block_index) * TILE_SIDE_BINS
        return (row_begin, row_begin + diag_id * spanned_columns)

    def accumulate(totals, gradient_extended, interior_maps, block_index):
        grads, conv_sum = totals
        row_begin, column_begin = anchor(block_index)
        local_gradients = gradient_extended[
            :,
            DILATION_STEP : DILATION_STEP + TILE_SIDE_BINS,
            DILATION_STEP : DILATION_STEP + spanned_columns,
        ]
        pair_grad = conv_transpose(
            gradient_extended, convolution_weight, TILE_SIDE_BINS, spanned_columns
        )
        row_cell_ids = row_begin + jnp.arange(TILE_SIDE_BINS, dtype=jnp.int32)
        column_cell_ids = column_begin + jnp.arange(spanned_columns, dtype=jnp.int32)
        pair_grad = jnp.where(
            grid_cells(row_cell_ids, column_cell_ids, block_total)[None], pair_grad, 0.0
        )
        row_code_values = lax.dynamic_slice_in_dim(
            padded_codes, row_begin + 2 * DILATION_STEP, TILE_SIDE_BINS, 0
        ).astype(jnp.float32)
        column_codes = lax.dynamic_slice_in_dim(
            padded_codes, column_begin + 2 * DILATION_STEP, spanned_columns, 0
        ).astype(jnp.float32)
        row_terms = jnp.concatenate(
            [
                jnp.sum(pair_grad, axis=2).T,
                jnp.einsum(
                    "cpq,qc->pc", pair_grad, column_codes[:, C:], precision=lax.Precision.HIGHEST
                ),
            ],
            axis=1,
        )
        col_terms = jnp.concatenate(
            [
                jnp.sum(pair_grad, axis=1).T,
                jnp.einsum(
                    "cpq,pc->qc", pair_grad, row_code_values[:, C:], precision=lax.Precision.HIGHEST
                ),
            ],
            axis=1,
        )
        grads = lax.dynamic_update_slice_in_dim(
            grads,
            lax.dynamic_slice_in_dim(grads, row_begin, TILE_SIDE_BINS, 0) + row_terms,
            row_begin,
            0,
        )
        grads = lax.dynamic_update_slice_in_dim(
            grads,
            lax.dynamic_slice_in_dim(grads, column_begin, spanned_columns, 0) + col_terms,
            column_begin,
            0,
        )
        tap_terms = []
        for tap_index in range(9):
            kernel_tap_row = tap_index // 3
            kernel_tap_column = tap_index % 3
            displaced_maps = interior_maps[
                :,
                DILATION_STEP * kernel_tap_row : DILATION_STEP * kernel_tap_row + TILE_SIDE_BINS,
                DILATION_STEP * kernel_tap_column : DILATION_STEP * kernel_tap_column
                + spanned_columns,
            ]
            tap_terms.append(
                jnp.einsum(
                    "opq,cpq->oc",
                    local_gradients,
                    displaced_maps,
                    preferred_element_type=jnp.float32,
                )
            )
        return (grads, conv_sum + jnp.stack(tap_terms, axis=0))

    start = (
        jnp.zeros((bins_total + BAND_TILE_COUNT * TILE_SIDE_BINS, 2 * C), jnp.float32),
        jnp.zeros((9, C, C), jnp.float32),
    )

    def forward_own(inputs):
        block_index, target_rows = inputs
        row_begin, column_begin = anchor(block_index)
        pairwise_maps = build_pair_maps(
            padded_codes,
            row_begin,
            column_begin,
            TILE_SIDE_BINS,
            spanned_columns,
            DILATION_STEP,
            block_total,
        )
        convolution_output = convolution_forward(
            pairwise_maps, convolution_weight, convolution_bias, TILE_SIDE_BINS, spanned_columns
        )
        row_cell_ids = row_begin + jnp.arange(TILE_SIDE_BINS, dtype=jnp.int32)
        column_cell_ids = column_begin + jnp.arange(spanned_columns, dtype=jnp.int32)
        mask = loss_cells(row_cell_ids, column_cell_ids, band_reach, block_total)
        return (
            head_grads(convolution_output, target_rows.astype(jnp.float32), mask, readout),
            pairwise_maps,
        )

    own_maps, maps_all = lax.map(forward_own, (block_ids, targets))
    grads_ext = extend_rims(own_maps)

    def section(totals, inputs):
        block_index, gradient_extended, interior_maps = inputs
        return (accumulate(totals, gradient_extended, interior_maps, block_index), None)

    (grads, conv_sum), _ = lax.scan(section, start, (block_ids, grads_ext, maps_all))
    grads_bin = grads[:bins_total]
    grads_store = jnp.take(
        grads_bin.reshape(block_total, TILE_SIDE_BINS, 2 * C), block_order, axis=0
    ).reshape(bins_total, 2 * C)
    conv_flat = (conv_sum / block_total).reshape(-1)
    codes_grad, conv_grad = (
        lax.psum_scatter(grads_store, ("row", "diag"), scatter_dimension=0, tiled=True),
        lax.psum_scatter(conv_flat, ("row", "diag"), scatter_dimension=0, tiled=True),
    )
    return (codes_grad, conv_grad)


def solution(mesh):
    in_specs = (P(("row", "diag"), None), P(), P(), P(), P(), P("row", None, "diag"), P(), P())
    out_specs = (P(("row", "diag"), None), P(("row", "diag")))
    return jax.shard_map(
        per_device, mesh=mesh, in_specs=in_specs, out_specs=out_specs, check_vma=False
    )
```

profile of v0, /device:TPU:0, one launch (start us, length us, event | category | flops | bytes accessed | tf_op | source)
XLA Modules:
  0.0 1514.1 jit_solution(15544249798769484867)
XLA Ops:
  10.4 196.9 %all-gather.2.cloned.1.call-done = bf16[8192,64]{1,0:T(8,128)(2,1)} async-done(((bf16[64,64]{1,0:T(8,128)(2,1)}), bf16[8192,64]{1,0:T(8,128)(2,1)}) %all-gather.2.cloned.1.call-update) | async-done | bytes 1048592 | tf_op jit(solution)/shard_map/all_gather | solution.py:170
  207.3 2.5 gather_fusion
  209.8 4.3 bitcast_select_fusion.1
  214.1 2.4 pad.4
  216.6 3.0 copy.66
  219.6 128.0 %while.33 = (s32[]{:T(128)}, bf16[8,32,128,128]{3,1,2,0:T(8,128)(2,1)}, bf16[8,32,160,160]{3,2,1,0:T(8,128)(2,1)}, f32[32]{0:T(128)S(1)}, s32[8]{0:T(128)S(1)}, ...) while((s32[]{:T(128)}, ...), condition=%wide.region_4.5_spmd, body=%wide.region_1.0_spmd.sunk | while | flops 324260864 | bytes 53484404 | solution.py:288
  232.7 2.9 fusion.251
  248.7 3.0 fusion.251
  264.7 2.9 fusion.251
  280.7 3.0 fusion.251
  296.7 2.9 fusion.251
  312.7 3.0 fusion.251
  328.7 2.9 fusion.251
  344.7 3.0 fusion.251
  347.6 12.8 copy.67
  360.4 3.0 fusion.132
  367.1 12.6 copy.69
  379.7 12.7 copy.70
  392.4 5.9 pad_maximum_fusion.9
  399.6 14.8 collective-permute-start.3
  422.3 3.1 collective-permute-start.4
  427.9 4.1 collective-permute-done.4
  432.0 4.4 collective-permute-done.5
  436.4 2.4 fusion.128
  438.8 32.2 %pad_maximum_fusion = bf16[8,32,160,160]{3,1,2,0:T(8,128)(2,1)} fusion(bf16[8,32,16,160]{3,1,2,0:T(8,128)(2,1)} %get-tuple-element.748, bf16[8,32,128,16]{3,1,2,0:T(8,128)(2,1)} %copy.70, bf16[8,32,128,128]{3,1,2,0:T(8,128)(2,1)} %get-tuple-element.472, bf16[8,32,128,16]{3,1,2,0:T(8,128)(2,1)} %copy.69, bf16[8,32,16,160]{3,1,2,0:T(8,128)(2,1)} %get-tuple-element.747), kind=kLoop, calls=%fused_computation.203 | loop fusion | flops 65536000 | bytes 26214400 | tf_op jit(solution)/shard_map/concatenate | solution.py:148
  471.0 2.6 broadcast_in_dim.177
  473.6 319.6 %while.34 = (s32[]{:T(128)}, f32[10240,64]{1,0:T(8,128)}, f32[9,32,32]{2,1,0:T(8,128)S(1)}, s32[8]{0:T(128)S(1)}, s32[]{:T(128)}, /*index=5*/s32[]{:T(128)}, bf1...) while((s32[]{:T(128)}, f32[10240,64]{1,0:T(8,128)}, ...), condition=%wide.region_8.9_spmd.clone, body=%wide.region_5.8_spmd.clone.sunk | while | flops 617236992 | bytes 116677656 | solution.py:295
  473.8 2.9 constant_dynamic-slice_fusion.2
  476.7 3.4 copy_bitcast_fusion.2
  498.2 5.7 copy.110
  508.2 5.4 copy.114
  513.7 2.9 constant_dynamic-slice_fusion.2
  516.5 3.4 copy_bitcast_fusion.2
  538.1 5.7 copy.110
  548.1 5.4 copy.114
  553.6 2.9 constant_dynamic-slice_fusion.2
  556.4 3.4 copy_bitcast_fusion.2
  578.0 5.7 copy.110
  588.0 5.4 copy.114
  593.4 2.9 constant_dynamic-slice_fusion.2
  596.3 3.4 copy_bitcast_fusion.2
  617.9 5.7 copy.110
  627.9 5.4 copy.114
  633.3 2.9 constant_dynamic-slice_fusion.2
  636.2 3.4 copy_bitcast_fusion.2
  657.8 5.7 copy.110
  667.8 5.4 copy.114
  673.2 2.9 constant_dynamic-slice_fusion.2
  676.1 3.4 copy_bitcast_fusion.2
  697.7 5.7 copy.110
  707.7 5.4 copy.114
  713.1 2.9 constant_dynamic-slice_fusion.2
  716.0 3.4 copy_bitcast_fusion.2
  737.6 5.7 copy.110
  747.6 5.4 copy.114
  753.0 2.9 constant_dynamic-slice_fusion.2
  755.9 3.4 copy_bitcast_fusion.2
  777.5 5.7 copy.110
  787.5 5.4 copy.114
  793.1 4.4 slice.469
  797.6 2.8 copy.74
  804.4 2.7 copy.88
  807.3 122.4 %all-reduce.1 = f32[9216]{0:T(1024)S(1)} all-reduce(f32[9216]{0:T(1024)S(1)} %reshape.640), channel_id=3, replica_groups=mesh['row'=8,'diag'=16] {'row','diag'}, use_global_device_ids=true, to_apply=%region_10.11.clone | all-reduce | flops 9216 | bytes 73728
  930.3 576.5 %reduce-scatter.4.cloned.1.call-done = f32[64,64]{1,0:T(8,128)} async-done(((f32[8192,64]{1,0:T(8,128)}), f32[64,64]{1,0:T(8,128)}) %reduce-scatter.4.cloned.1.call-update) | async-done | bytes 16400
  (566 shorter events, 294.6 us)
Async XLA Ops:
  7.2 0.8 copy-start
  7.2 200.1 %all-gather.2.cloned.1.call-start = ((), (), s32[]{:S(2)}) async-start(), calls=%async_computation.1 | async-start | bytes 2113536 | tf_op jit(solution)/shard_map/all_gather | solution.py:170
  9.5 1497.3 %reduce-scatter.4.cloned.1.call-start = ((), (), s32[]{:S(2)}) async-start(), calls=%async_computation.2 | async-start | bytes 4227072
  216.5 3.1 copy-start.6
  216.5 3.1 copy-start.7
  216.6 3.1 copy-start.9
  216.6 3.0 copy-start.10
  363.4 3.7 collective-permute-start
  365.6 14.1 collective-permute-start.1
  392.4 22.1 %copy-start.11 = (s32[64]{0:T(128)S(1)}, s32[64]{0:T(128)}, u32[]{:S(2)}) copy-start(s32[64]{0:T(128)} %param.18) | copy-start | bytes 772
  398.3 16.8 %collective-permute-start.2 = (bf16[8,1,32,16,160]{4,2,3,0,1:T(8,128)(2,1)}, bf16[8,1,32,16,160]{4,2,3,0,1:T(8,128)(2,1)}, u32[]{:S(2)}, u32[]{:S(2)}) collective-permute-start(bf16[8,1,32,16,160]{4,2,3,0,1:T(8,128)(2,1)} %bitcast.35), channel_id=1, source_target_pairs={{1,0},{2,1},{3,2},{4,3},{5,4},{6,5},{7,6},{8,7},{9,8},{10,9},{11,1... | collective-permute-start | bytes 3932168 | tf_op jit(solution)/shard_map/ppermute | solution.py:24
  399.6 19.6 %collective-permute-start.3 = (bf16[8,1,32,16,160]{4,2,3,0,1:T(8,128)(2,1)}, bf16[8,1,32,16,160]{4,2,3,0,1:T(8,128)(2,1)}, u32[]{:S(2)}, u32[]{:S(2)}) collective-permute-start(bf16[8,1,32,16,160]{4,2,3,0,1:T(8,128)(2,1)} %bitcast.38), channel_id=1, source_target_pairs={{0,1},{1,2},{2,3},{3,4},{4,5},{5,6},{6,7},{7,8},{8,9},{9,10},{10,1... | collective-permute-start | bytes 3932168 | tf_op jit(solution)/shard_map/ppermute | solution.py:23
  422.3 9.7 collective-permute-start.4
  425.3 11.1 collective-permute-start.5
  473.8 2.9 copy-start.4
  495.2 1.4 copy-start.2
  498.2 6.4 copy-start.3
  508.2 5.4 copy-start.5
  513.7 2.9 copy-start.4
  535.1 1.4 copy-start.2
  538.1 6.4 copy-start.3
  548.1 5.4 copy-start.5
  553.6 2.9 copy-start.4
  575.0 1.4 copy-start.2
  578.0 6.4 copy-start.3
  588.0 5.4 copy-start.5
  593.4 2.9 copy-start.4
  614.8 1.4 copy-start.2
  617.9 6.4 copy-start.3
  627.9 5.4 copy-start.5
  633.3 2.9 copy-start.4
  654.7 1.4 copy-start.2
  657.8 6.4 copy-start.3
  667.8 5.4 copy-start.5
  673.2 2.9 copy-start.4
  694.6 1.4 copy-start.2
  697.7 6.4 copy-start.3
  707.7 5.4 copy-start.5
  713.1 2.9 copy-start.4
  734.5 1.4 copy-start.2
  737.6 6.4 copy-start.3
  747.6 5.4 copy-start.5
  753.0 2.9 copy-start.4
  774.4 1.4 copy-start.2
  777.5 6.4 copy-start.3
  787.5 5.4 copy-start.5
  800.4 2.3 copy-start.8
  804.4 702.3 %copy-start.1 = (bf16[64,256]{1,0:T(8,128)(2,1)S(1)}, bf16[64,256]{1,0:T(8,128)(2,1)}, u32[]{:S(2)}) copy-start(bf16[64,256]{1,0:T(8,128)(2,1)} %param.12) | copy-start | bytes 98308
Sparse Core Ops, SparseCore 0:
  10.3 196.9 all-gather.1
  807.3 699.4 reduce-scatter.3
where the time goes:
time: 1530 us; the launch traced here: 1510 us
  waiting for transfers between devices  782 us (51%)
  local copies, waits for them, and re-layouts  238 us (16%)
  matrix products  165 us (11%)
  other arithmetic  154 us (10%)
  blocking collectives  122 us (8%)
  starting transfers between devices  24.2 us (2%)
    unnamed x3, waiting for transfers between devices  577 us
    all_gather x1, waiting for transfers between devices, per_device(): code_rows = lax.all_gather(code_local, ('row', 'diag'), axis=0, tiled=True)  197 us
    unnamed x1, blocking collectives  122 us
    while x88, local copies, waits for them, and re-layouts  101 us
    dot_general x72, matrix products, accumulate(): jnp.einsum('opq,cpq->oc', local_gradients, displaced_maps, preferred_elem...  56.1 us
    dot_general x72, matrix products, convolution_forward(): jnp.einsum('oc,cpq->opq', weights[tap_index], displaced_maps, preferred_e...  45.8 us
    dot_general x72, matrix products, conv_transpose(): jnp.einsum('oc,opq->cpq', weights[tap_index], displaced_maps, preferred_e...  43.2 us
    dynamic_update_slice x16, other arithmetic, per_device(): own_maps, maps_all = lax.map(forward_own, (block_ids, targets))  38.1 us
  transfers between devices with their start and end apart: 8, of which 5 were waited for; matrix products, arithmetic and copies ran while one was open for 1% of the time, Pallas kernels for 0%

commit v1 on v0

v1 whole, which is shorter than its diff:
```python
import functools

import jax
import jax.numpy as jnp
from jax import lax
from jax.experimental import pallas as pl
from jax.experimental.pallas import tpu as pltpu
from jax.sharding import PartitionSpec as P

C = 32
TILE = 128
STEP = 16
BAND = 16
GROUPS = TILE // STEP
PAIRS = GROUPS // 2
SLABS = GROUPS + 2
SPAN = TILE + 2 * STEP
PLANE = PAIRS * STEP
ROWS = STEP * PLANE
CHUNK = 512

SQRT_HALF = 0.7071067811865476
INV_SQRT_TAU = 0.3989422804014327
BF = jnp.bfloat16
F32 = jnp.float32


def dot(a, b, dims=(((1,), (0,)), ((), ()))):
    return lax.dot_general(a, b, dims, preferred_element_type=F32)


def lane_fold(x):
    x = x + pltpu.roll(x, 64, 1)
    return x + pltpu.roll(x, 32, 1)


def tile_kernel(
    blocks,
    tiles,
    s_ref,
    row_prev,
    row_here,
    row_next,
    col_prev,
    col_here,
    col_next,
    tgt_ref,
    wf_ref,
    wb_ref,
    spread_ref,
    ones_ref,
    place_ref,
    vec_ref,
    grads_ref,
    taps_ref,
    u_row,
    w_row,
    uq_s,
    wq_s,
    mask_s,
    dist_s,
    x_s,
    r0_s,
    r1_s,
    c0_s,
    c1_s,
    acc_s,
    row_acc,
    col_acc,
):
    t = pl.program_id(0)
    a = s_ref[2 * blocks] * tiles + t
    d = s_ref[2 * blocks + 1]
    b = a + d
    reach = s_ref[blocks + a]

    @pl.when(t == 0)
    def _():
        acc_s[...] = jnp.zeros_like(acc_s)
        row_acc[...] = jnp.zeros_like(row_acc)
        col_acc[...] = jnp.zeros_like(col_acc)
        line = lax.broadcasted_iota(jnp.int32, (ROWS, 256), 0)
        lane = lax.broadcasted_iota(jnp.int32, (ROWS, 256), 1)
        r = line // PLANE
        jp = (line % PLANE) // STEP
        s = line % STEP
        ii = lane // 64
        jj = (lane // 32) % 2
        dist_s[...] = 32 * jp + s - r + 16 * (jj - ii)

    def codes(prev, here, after):
        left, right = spread_ref[0], spread_ref[1]
        return jnp.concatenate(
            [
                dot(prev[0], right),
                dot(here[0], left),
                dot(here[0], right),
                dot(here[1], left),
                dot(here[1], right),
                dot(after[0], left),
            ],
            axis=0,
        )

    row_codes = codes(row_prev, row_here, row_next)
    u_row[...] = row_codes[:, :128]
    w_row[...] = row_codes[:, 128:]
    col_codes = codes(col_prev, col_here, col_next).reshape(SLABS, STEP, 256)
    group = lax.broadcasted_iota(jnp.int32, (STEP, 256), 1) // C % 4
    for jp in range(PAIRS):
        window = col_codes[2 * jp]
        for g in range(1, 4):
            window = jnp.where(group == g, col_codes[2 * jp + g], window)
        uq_s[jp * STEP : (jp + 1) * STEP, :] = window[:, :128]
        wq_s[jp * STEP : (jp + 1) * STEP, :] = window[:, 128:]

    line = lax.broadcasted_iota(jnp.int32, (PLANE, 128), 0)
    lane = lax.broadcasted_iota(jnp.int32, (PLANE, 128), 1)
    at_left = (line < STEP) & (lane < C)
    at_right = (line >= PLANE - STEP) & (lane >= 3 * C)
    for k in range(3):
        ar = a - 1 + k

        def inside(cb):
            ok = (ar >= 0) & (ar < blocks) & (cb >= ar) & (cb - ar < BAND) & (cb < blocks)
            return jnp.where(ok, 1.0, 0.0).astype(F32)

        mask_s[k] = jnp.where(
            at_left, inside(b - 1), jnp.where(at_right, inside(b + 1), inside(b))
        )

    uq = uq_s[...]
    wq = wq_s[...]

    def kind(i):
        return 0 if i == 0 else (2 if i == SLABS - 1 else 1)

    def make_maps(r, carry):
        for i in range(SLABS):
            u = u_row[pl.ds(i * STEP + r, 1), :]
            w = w_row[pl.ds(i * STEP + r, 1), :]
            value = ((u + uq) + w * wq) * mask_s[kind(i)]
            x_s[i, pl.ds(pl.multiple_of(r * PLANE, PLANE), PLANE), :] = value.astype(BF)
        return carry

    lax.fori_loop(0, STEP, make_maps, 0)

    c0_s[...] = jnp.zeros_like(c0_s)
    c1_s[...] = jnp.zeros_like(c1_s)
    bias = vec_ref[0:1, :]
    read = vec_ref[1:2, :]
    read_density = read * INV_SQRT_TAU
    planes = CHUNK // PLANE

    def step(ch, carry):
        r0 = ch * planes
        at = pl.multiple_of(ch * CHUNK, CHUNK)
        rows = pl.ds(at, CHUNK)
        grads = []
        for ig in range(2):
            maps = jnp.concatenate([x_s[4 * ig + i, rows, :] for i in range(6)], axis=1)
            v = dot(maps, wf_ref[...]) + bias
            cdf = 0.5 * (1.0 + lax.erf(v * SQRT_HALF))
            density = jnp.exp(-0.5 * v * v)
            read_cdf = read * cdf
            g = v * read_cdf
            high = g.astype(BF)
            low = (g - high.astype(F32)).astype(BF)
            pred = dot(high, ones_ref[...]) + dot(low, ones_ref[...])
            target = dot(tgt_ref[0, rows, :], place_ref[ig])
            lowest = 64 * ig - TILE * d
            highest = jnp.where(b < blocks, reach + lowest, -100000)
            dist = dist_s[rows, :]
            keep = (dist >= lowest) & (dist <= highest)
            err = jnp.where(keep, pred - target, 0.0) * TILE ** (-0.5)
            grad = (err * (read_cdf + read_density * (v * density))).astype(BF)
            grads.append(grad)
            acc_s[...] += dot(grad, maps, (((0,), (0,)), ((), ())))
        for k in range(SLABS // 2):
            total = None
            for ig in range(2):
                slot = k - 2 * ig
                if 0 <= slot < 3:
                    part = dot(grads[ig], wb_ref[:, 256 * slot : 256 * (slot + 1)])
                    total = part if total is None else total + part
            for half in range(2):
                i = 2 * k + half
                dx = total[:, 128 * half : 128 * (half + 1)].reshape(planes, PLANE, 128)
                dx = dx * mask_s[kind(i)][None]
                dxw = dx * wq_s[...][None]
                for rr in range(planes):
                    p = i * STEP + r0 + rr
                    r0_s[p] = jnp.sum(dx[rr].reshape(PLANE // 8, 8, 128), axis=0)
                    r1_s[p] = jnp.sum(dxw[rr].reshape(PLANE // 8, 8, 128), axis=0)
                    c0_s[...] += dx[rr]
                    c1_s[...] += dx[rr] * w_row[pl.ds(p, 1), :]
        return carry

    lax.fori_loop(0, ROWS // CHUNK, step, 0)

    lanes = lax.broadcasted_iota(jnp.int32, (SPAN, 128), 1)
    even = lanes // C % 2 == 0
    row_terms = jnp.where(
        even,
        lane_fold(jnp.sum(r0_s[...], axis=1)),
        lane_fold(jnp.sum(r1_s[...], axis=1)),
    )
    here = pl.ds(pl.multiple_of(t * TILE, TILE), SPAN)
    row_acc[here, :] += row_terms

    group = lax.broadcasted_iota(jnp.int32, (STEP, 128), 1) // C

    def unwind(ref):
        parts = []
        for m in range(PAIRS + 1):
            for odd in range(2):
                value = jnp.zeros((STEP, 128), F32)
                if m < PAIRS:
                    value = jnp.where(group == odd, ref[m * STEP : (m + 1) * STEP, :], value)
                if m > 0:
                    value = jnp.where(group == 2 + odd, ref[(m - 1) * STEP : m * STEP, :], value)
                parts.append(value)
        return lane_fold(jnp.concatenate(parts, axis=0))

    col_acc[here, :] += jnp.where(even, unwind(c0_s), unwind(c1_s))

    @pl.when(t == tiles - 1)
    def _():
        grads_ref[...] = jnp.zeros_like(grads_ref)
        first = s_ref[2 * blocks] * tiles
        low_half = lax.broadcasted_iota(jnp.int32, (32, 128), 1) < 64

        def put(acc_ref, base, k, begin, count):
            n = base + k

            @pl.when((n >= 0) & (n < blocks))
            def _():
                slot = s_ref[n]
                for h in range(2):
                    top = acc_ref[pl.ds(begin + 64 * h, 32), :]
                    bottom = acc_ref[pl.ds(begin + 64 * h + 32, 32), :]
                    grads_ref[2 * slot + h] += jnp.where(low_half, top, bottom)

        for acc_ref, base in ((row_acc, first), (col_acc, first + d)):
            for k in range(tiles):
                put(acc_ref, base, k, STEP + k * TILE, TILE)

            @pl.when((base > 0) & (base <= blocks))
            def _():
                slot = s_ref[jnp.clip(base - 1, 0, blocks - 1)]
                grads_ref[2 * slot + 1, pl.ds(16, 16), :] += jnp.where(
                    low_half[:16], 0.0, acc_ref[0:STEP, :]
                )

            @pl.when(base + tiles < blocks)
            def _():
                slot = s_ref[jnp.minimum(base + tiles, blocks - 1)]
                grads_ref[2 * slot, pl.ds(0, 16), :] += jnp.where(
                    low_half[:16], acc_ref[STEP + tiles * TILE : 2 * STEP + tiles * TILE, :], 0.0
                )

        for ty in range(3):
            total = acc_s[0:64, 128 * ty : 128 * (ty + 1)]
            for ii in range(1, 4):
                total = total + acc_s[
                    64 * ii : 64 * (ii + 1), 128 * (ii + ty) : 128 * (ii + ty + 1)
                ]
            taps_ref[ty] = total[:C] + pltpu.roll(total[C:], 96, 1)


def run_tiles(scalars, code_chunks, tgt, wf, wb, vec, blocks, tiles):
    lane = jnp.arange(256, dtype=jnp.int32)
    source = lane // 128 * C + lane % C
    depth = jnp.arange(128, dtype=jnp.int32)
    spread = jnp.stack(
        [depth[:, None] == source[None, :], depth[:, None] == 64 + source[None, :]]
    ).astype(BF)
    ones = (lane[:, None] // C == lane[None, :] // C).astype(BF)
    sixteen = jnp.arange(16, dtype=jnp.int32)
    place = jnp.stack(
        [sixteen[:, None] == 8 * ig + lane[None, :] // C for ig in range(2)]
    ).astype(BF)

    def chunk_spec(offset, column, edge):
        def index(t, s):
            n = s[2 * blocks] * tiles + t + offset
            if column:
                n = n + s[2 * blocks + 1]
            n = s[jnp.clip(n, 0, blocks - 1)]
            if edge < 0:
                return (2 * n + 1, 1, 0)
            if edge > 0:
                return (2 * n, 0, 0)
            return (n, 0, 0)

        return pl.BlockSpec((1, STEP, 128) if edge else (2, 32, 128), index)

    def whole(x):
        zeros = (0,) * x.ndim
        return pl.BlockSpec(x.shape, lambda t, s: zeros)

    grid_spec = pltpu.PrefetchScalarGridSpec(
        num_scalar_prefetch=1,
        grid=(tiles,),
        in_specs=[
            chunk_spec(-1, False, -1),
            chunk_spec(0, False, 0),
            chunk_spec(1, False, 1),
            chunk_spec(-1, True, -1),
            chunk_spec(0, True, 0),
            chunk_spec(1, True, 1),
            pl.BlockSpec((1, ROWS, 16), lambda t, s: (t, 0, 0)),
            whole(wf),
            whole(wb),
            whole(spread),
            whole(ones),
            whole(place),
            whole(vec),
        ],
        out_specs=[
            pl.BlockSpec((2 * blocks, 32, 128), lambda t, s: (0, 0, 0)),
            pl.BlockSpec((3, C, 128), lambda t, s: (0, 0, 0)),
        ],
        scratch_shapes=[
            pltpu.VMEM((SPAN, 128), F32),
            pltpu.VMEM((SPAN, 128), F32),
            pltpu.VMEM((PLANE, 128), F32),
            pltpu.VMEM((PLANE, 128), F32),
            pltpu.VMEM((3, PLANE, 128), F32),
            pltpu.VMEM((ROWS, 256), jnp.int32),
            pltpu.VMEM((SLABS, ROWS, 128), BF),
            pltpu.VMEM((SPAN, 8, 128), F32),
            pltpu.VMEM((SPAN, 8, 128), F32),
            pltpu.VMEM((PLANE, 128), F32),
            pltpu.VMEM((PLANE, 128), F32),
            pltpu.VMEM((256, 768), F32),
            pltpu.VMEM((tiles * TILE + 2 * STEP, 128), F32),
            pltpu.VMEM((tiles * TILE + 2 * STEP, 128), F32),
        ],
    )
    return pl.pallas_call(
        functools.partial(tile_kernel, blocks, tiles),
        grid_spec=grid_spec,
        out_shape=[
            jax.ShapeDtypeStruct((2 * blocks, 32, 128), F32),
            jax.ShapeDtypeStruct((3, C, 128), F32),
        ],
        compiler_params=pltpu.CompilerParams(
            dimension_semantics=("arbitrary",), vmem_limit_bytes=48 * 1024 * 1024
        ),
    )(
        scalars,
        code_chunks,
        code_chunks,
        code_chunks,
        code_chunks,
        code_chunks,
        code_chunks,
        tgt,
        wf,
        wb,
        spread,
        ones,
        place,
        vec,
    )


def per_device(
    bins_x,
    proj_weight,
    convolution_weight,
    convolution_bias,
    readout,
    targets,
    block_order,
    band_reach,
):
    tiles = targets.shape[0]
    blocks = block_order.shape[0]
    axes = ("row", "diag")
    code_local = dot(bins_x, proj_weight).astype(BF)
    packed = jnp.concatenate([code_local[:32], code_local[32:]], axis=1)
    code_chunks = lax.all_to_all(
        jnp.broadcast_to(packed[None], (2 * blocks, 32, 128)), axes, 0, 0, tiled=True
    )
    positions = jnp.arange(blocks, dtype=jnp.int32)
    inverse = jnp.sum(
        jnp.where(block_order[:, None] == positions[None, :], positions[:, None], 0), axis=0
    )
    scalars = jnp.concatenate(
        [
            inverse,
            band_reach,
            jnp.stack([lax.axis_index("row"), lax.axis_index("diag")]).astype(jnp.int32),
        ]
    )
    tgt = (
        targets.reshape(tiles, GROUPS, STEP, PAIRS, 2, STEP)
        .transpose(0, 2, 3, 5, 1, 4)
        .reshape(tiles, ROWS, 2 * GROUPS)
    )
    taps = convolution_weight.reshape(3, 3, C, C).transpose(0, 1, 3, 2)
    wf = jnp.stack(
        [
            jnp.pad(taps, ((ii, 3 - ii), (jj, 1 - jj), (0, 0), (0, 0)))
            for ii in range(4)
            for jj in range(2)
        ],
        axis=3,
    ).reshape(768, 256)
    wb = wf.T
    vec = jnp.stack([jnp.tile(convolution_bias, 8), jnp.tile(readout, 8)])
    grads, tap_sums = run_tiles(scalars, code_chunks, tgt, wf, wb, vec, blocks, tiles)
    tap_flat = (
        tap_sums[:, :, : 3 * C].reshape(3, C, 3, C).transpose(0, 2, 1, 3).reshape(2 * blocks, -1)
        / blocks
    )
    owned = tap_flat.shape[1]
    tap_rows = jnp.pad(tap_flat, ((0, 0), (0, 1024 - owned))).reshape(2 * blocks, 8, 128)
    terms = jnp.concatenate([grads.astype(BF), tap_rows.astype(BF)], axis=1)
    received = lax.all_to_all(terms, axes, 0, 0, tiled=True)
    mine = jnp.sum(received.astype(F32), axis=0)
    codes_grad = jnp.concatenate([mine[:32, :64], mine[:32, 64:]], axis=0)
    conv_grad = mine[32, :owned]
    return (codes_grad, conv_grad)


def solution(mesh):
    in_specs = (P(("row", "diag"), None), P(), P(), P(), P(), P("row", None, "diag"), P(), P())
    out_specs = (P(("row", "diag"), None), P(("row", "diag")))
    return jax.shard_map(
        per_device, mesh=mesh, in_specs=in_specs, out_specs=out_specs, check_vma=False
    )
```

time: 1530 us -> 132 us (0.09)
  waiting for transfers between devices: 782 us -> 3.54 us
  local copies, waits for them, and re-layouts: 238 us -> 17.9 us
  matrix products: 165 us -> 0.88 us
  other arithmetic: 154 us -> 1.73 us
  blocking collectives: 122 us -> 28.1 us
  Pallas kernels: 0 us -> 66.8 us
    unnamed x3 -> x0, waiting for transfers between devices: 577 us -> none
    all_gather x1 -> x0, waiting for transfers between devices: 197 us -> none  [per_device(): code_rows = lax.all_gather(code_local, ('row', 'diag'), axis=0, tiled=True)]
    dot_general x225 -> x1, matrix products: 165 us -> 0.88 us  [dot(): return lax.dot_general(a, b, dims, preferred_element_type=F32)]
    unnamed x1 -> x0, blocking collectives: 122 us -> none
    while x90 -> x0, local copies, waits for them, and re-layouts: 116 us -> none
    pallas_call x0 -> x1, Pallas kernels: none -> 66.8 us  [run_tiles(): pl.pallas_call(functools.partial(tile_kernel, blocks, tiles), grid_spec=g...]
    dynamic_update_slice x24 -> x0, other arithmetic: 49.2 us -> none  [the longest x16 38.1 us: per_device(): own_maps, maps_all = lax.map(forward_own, (block_ids, targets))]
    dynamic_slice x24 -> x0, local copies, waits for them, and re-layouts: 32.9 us -> none  [the longest x8 22.9 us: per_device(): lax.scan(section, start, (block_ids, grads_ext, maps_all))]
  transfers between devices with their start and end apart: 8 -> 1, of which waited for: 5 -> 1; matrix products, arithmetic and copies ran while one was open for 1% -> 12% of each run, Pallas kernels for 0% -> 0%
where the time goes in v1:
time: 132 us; the launch traced here: 131 us
  Pallas kernels  66.8 us (51%)
  blocking collectives  28.1 us (21%)
  local copies, waits for them, and re-layouts  17.9 us (14%)
  starting transfers between devices  11.1 us (8%)
  waiting for transfers between devices  3.54 us (3%)
  other arithmetic  1.73 us (1%)
    pallas_call x1, Pallas kernels, run_tiles(): pl.pallas_call(functools.partial(tile_kernel, blocks, tiles), grid_spec=g...  66.8 us
    all_to_all x1, blocking collectives, per_device(): received = lax.all_to_all(terms, axes, 0, 0, tiled=True)  28.1 us
    all_to_all x1, starting transfers between devices, per_device(): lax.all_to_all(jnp.broadcast_to(packed[None], (2 * blocks, 32, 128)), axe...  11.1 us
    reshape x2, local copies, waits for them, and re-layouts, per_device(): tgt = targets.reshape(tiles, GROUPS, STEP, PAIRS, 2, STEP).transpose(0, 2...  6.46 us
    reshape x2, local copies, waits for them, and re-layouts, per_device(): targets.reshape(tiles, GROUPS, STEP, PAIRS, 2, STEP)  6.41 us
    all_to_all x1, waiting for transfers between devices, per_device(): lax.all_to_all(jnp.broadcast_to(packed[None], (2 * blocks, 32, 128)), axe...  3.54 us
  transfers between devices with their start and end apart: 1, of which 1 were waited for; matrix products, arithmetic and copies ran while one was open for 12% of the time, Pallas kernels for 0%

profile of v1, /device:TPU:0, one launch (start us, length us, event | category | flops | bytes accessed | tf_op | source)
XLA Modules:
  0.0 131.0 jit_solution(5124217312724691214)
XLA Ops:
  0.6 0.0 copy-start
  0.6 0.7 copy-done
  1.4 0.9 convolution_convert_fusion
  2.3 0.1 pad_maximum_fusion.2
  2.4 0.0 copy-start.6
  2.4 0.0 copy-start.2
  2.4 1.1 broadcast_in_dim.16
  3.5 11.1 %all-to-all-start = ((bf16[128,32,128]{2,1,0:T(8,128)(2,1)}), bf16[128,32,128]{2,1,0:T(8,128)(2,1)S(1)}, u32[]{:S(2)}, u32[]{:S(2)}) async-start(bf16[128,32,128]{2,1,0:T(8,128)(2,1)} %broadcast_in_dim.16), calls=%async_computation | async-start | bytes 2097152 | tf_op jit(solution)/shard_map/all_to_all | solution.py:384
  14.6 0.0 copy-start.5
  14.6 0.0 copy-start.3
  14.7 0.0 copy-start.4
  14.7 0.0 copy-done.6
  14.7 0.1 select_reduce_fusion
  14.8 0.0 copy-done.2
  14.8 0.1 copy.27
  14.9 0.1 bitcast_dynamic-update-slice_fusion.7
  15.0 0.1 bitcast_dynamic-update-slice_fusion.6
  15.1 0.1 bitcast_dynamic-update-slice_fusion.5
  15.2 0.1 bitcast_dynamic-update-slice_fusion.4
  15.3 0.1 bitcast_dynamic-update-slice_fusion.3
  15.4 0.1 bitcast_dynamic-update-slice_fusion.2
  15.5 0.1 bitcast_dynamic-update-slice_fusion.1
  15.6 0.0 copy-start.1
  15.6 0.1 bitcast_dynamic-update-slice_fusion
  15.7 0.0 copy-done.5
  15.7 0.1 pad_add_fusion.s_ref
  15.8 0.0 copy-done.3
  15.8 0.1 stack_tile.6
  15.9 0.0 copy-done.4
  15.9 0.1 stack_tile.7
  16.0 1.0 reshape.255
  17.0 0.2 copy.21.wf_ref
  17.2 0.0 copy-done.1
  17.2 2.4 %reshape.252 = bf16[8,8,16,4,2,16]{5,4,3,2,1,0:T(2,128)(2,1)} reshape(bf16[8,128,128]{2,1,0:T(8,128)(2,1)S(1)} %copy-done.1) | data formatting | bytes 524288 | tf_op jit(solution)/shard_map/reshape | solution.py:399
  19.6 4.0 %copy.26 = bf16[8,8,16,4,2,16]{5,3,2,4,1,0:T(4,128)(2,1)} copy(bf16[8,8,16,4,2,16]{5,4,3,2,1,0:T(2,128)(2,1)} %reshape.252) | data formatting | bytes 524288 | tf_op jit(solution)/shard_map/reshape | solution.py:399
  23.6 4.7 %reshape.253 = bf16[8,1024,16]{1,2,0:T(8,128)(2,1)S(1)} reshape(bf16[8,16,4,16,8,2]{3,2,1,5,4,0:T(4,128)(2,1)} %bitcast.41) | data formatting | bytes 524288 | tf_op jit(solution)/shard_map/reshape | solution.py:401
  28.3 1.8 %copy.20.tgt_ref = bf16[8,1024,16]{2,1,0:T(8,128)(2,1)} copy(bf16[8,1024,16]{1,2,0:T(8,128)(2,1)S(1)} %reshape.253) | data formatting | bytes 524288 | tf_op jit(solution)/shard_map/reshape | solution.py:401
  30.2 0.1 compare_convert_fusion.ones_ref
  30.3 3.5 %all-to-all-done.row_prev.row_here.row_next.col_prev.col_here.col_next = bf16[128,32,128]{2,1,0:T(8,128)(2,1)S(1)} async-done(((bf16[128,32,128]{2,1,0:T(8,128)(2,1)}), bf16[128,32,128]{2,1,0:T(8,128)(2,1)S(1)}, u32[]{:S(2)}, u32[]{:S(2)}) %all-to-all-start) | async-done | bytes 1048608 | tf_op jit(solution)/shard_map/all_to_all | solution.py:384
  33.8 66.8 %shard_map.95 = (f32[128,32,128]{2,1,0:T(8,128)S(1)}, f32[3,32,128]{2,1,0:T(8,128)S(1)}) custom-call(s32[130]{0:T(256)S(1)} %pad_add_fusion.s_ref, bf16[128,32,128]{2,1,0:T(8,128)(2,1)S(1)} %all-to-all-done.row_prev.row_here.row_next.col_prev.col_here.col_next, bf16[128,32,128]{2,1,0:T(8,128)(2,1)S(1)} %all-to-all-done.row_prev.row_here.row_next.col_prev.col_here.col_next, ...), custom_call_target="tpu_custom_call" | custom-call | tf_op jit(solution)/shard_map/pallas_call | solution.py:341
  100.7 0.2 convert_element_type.44
  100.9 0.1 div.48
  101.0 0.1 div.50
  101.3 0.2 pad_maximum_fusion
  101.4 28.1 %all_to_all.10 = bf16[128,40,128]{2,1,0:T(8,128)(2,1)S(1)} all-to-all(bf16[128,40,128]{2,1,0:T(8,128)(2,1)S(1)} %pad_maximum_fusion), channel_id=1, replica_groups=mesh['row'=8,'diag'=16] {'row','diag'}, dimensions={0} | all-to-all | bytes 2621440 | tf_op jit(solution)/shard_map/all_to_all | solution.py:422
  129.6 0.2 convert_reduce_fusion
  129.8 0.5 slice_bitcast_fusion
  130.3 0.1 fusion.5
  130.4 0.6 pad_maximum_fusion.1
  (16 shorter events, 0.2 us)
Async XLA Ops:
  0.6 0.8 copy-start
  2.4 12.4 %copy-start.6 = (s32[64]{0:T(128)S(1)}, s32[64]{0:T(128)}, u32[]{:S(2)}) copy-start(s32[64]{0:T(128)} %param.14) | copy-start | bytes 772
  2.4 12.5 %copy-start.2 = (bf16[9,32,32]{2,1,0:T(8,128)(2,1)S(1)}, bf16[9,32,32]{2,1,0:T(8,128)(2,1)}, u32[]{:S(2)}) copy-start(bf16[9,32,32]{2,1,0:T(8,128)(2,1)} %param.10) | copy-start | bytes 55300
  3.5 30.3 %all-to-all-start = ((bf16[128,32,128]{2,1,0:T(8,128)(2,1)}), bf16[128,32,128]{2,1,0:T(8,128)(2,1)S(1)}, u32[]{:S(2)}, u32[]{:S(2)}) async-start(bf16[128,32,128]{2,1,0:T(8,128)(2,1)} %broadcast_in_dim.16), calls=%async_computation | async-start | bytes 2097152 | tf_op jit(solution)/shard_map/all_to_all | solution.py:384
  14.6 1.1 copy-start.5
  14.6 1.2 copy-start.3
  14.7 1.2 copy-start.4
  15.6 1.6 %copy-start.1 = (bf16[8,128,128]{2,1,0:T(8,128)(2,1)S(1)}, bf16[8,128,128]{2,1,0:T(8,128)(2,1)}, u32[]{:S(2)}) copy-start(bf16[8,128,128]{2,1,0:T(8,128)(2,1)} %param.13) | copy-start | bytes 786436

commit v2 on v1

--- a/solution.py
+++ b/solution.py
@@ -11,13 +11,13 @@
 TILE = 128
 STEP = 16
 BAND = 16
-GROUPS = TILE // STEP
-PAIRS = GROUPS // 2
-SLABS = GROUPS + 2
+PAIRS = TILE // (2 * STEP)
+SLABS = TILE // STEP + 2
 SPAN = TILE + 2 * STEP
 PLANE = PAIRS * STEP
 ROWS = STEP * PLANE
 CHUNK = 512
+MPIECE = 512
 
 SQRT_HALF = 0.7071067811865476
 INV_SQRT_TAU = 0.3989422804014327
@@ -32,6 +32,15 @@
 def lane_fold(x):
     x = x + pltpu.roll(x, 64, 1)
     return x + pltpu.roll(x, 32, 1)
+
+
+def weave(*streams):
+    streams = [list(x) for x in streams if x]
+    order = sorted(
+        ((n + 0.5) / len(x), m, n) for m, x in enumerate(streams) for n in range(len(x))
+    )
+    for _, m, n in order:
+        streams[m][n]()
 
 
 def tile_kernel(
@@ -48,7 +57,6 @@
     wf_ref,
     wb_ref,
     spread_ref,
-    ones_ref,
     place_ref,
     vec_ref,
     grads_ref,
@@ -59,6 +67,7 @@
     wq_s,
     mask_s,
     dist_s,
+    tgt_s,
     x_s,
     r0_s,
     r1_s,
@@ -68,13 +77,13 @@
     row_acc,
     col_acc,
 ):
-    t = pl.program_id(0)
-    a = s_ref[2 * blocks] * tiles + t
+    g = pl.program_id(0)
+    new = g % 2
+    old = 1 - new
     d = s_ref[2 * blocks + 1]
-    b = a + d
-    reach = s_ref[blocks + a]
-
-    @pl.when(t == 0)
+    first = s_ref[2 * blocks] * tiles
+
+    @pl.when(g == 0)
     def _():
         acc_s[...] = jnp.zeros_like(acc_s)
         row_acc[...] = jnp.zeros_like(row_acc)
@@ -102,132 +111,263 @@
             axis=0,
         )
 
+    def kind(i):
+        return 0 if i == 0 else (2 if i == SLABS - 1 else 1)
+
     row_codes = codes(row_prev, row_here, row_next)
     u_row[...] = row_codes[:, :128]
-    w_row[...] = row_codes[:, 128:]
+    w_row[new] = row_codes[:, 128:]
     col_codes = codes(col_prev, col_here, col_next).reshape(SLABS, STEP, 256)
     group = lax.broadcasted_iota(jnp.int32, (STEP, 256), 1) // C % 4
     for jp in range(PAIRS):
         window = col_codes[2 * jp]
-        for g in range(1, 4):
-            window = jnp.where(group == g, col_codes[2 * jp + g], window)
+        for m in range(1, 4):
+            window = jnp.where(group == m, col_codes[2 * jp + m], window)
         uq_s[jp * STEP : (jp + 1) * STEP, :] = window[:, :128]
-        wq_s[jp * STEP : (jp + 1) * STEP, :] = window[:, 128:]
-
+        wq_s[new, jp * STEP : (jp + 1) * STEP, :] = window[:, 128:]
     line = lax.broadcasted_iota(jnp.int32, (PLANE, 128), 0)
     lane = lax.broadcasted_iota(jnp.int32, (PLANE, 128), 1)
     at_left = (line < STEP) & (lane < C)
     at_right = (line >= PLANE - STEP) & (lane >= 3 * C)
     for k in range(3):
-        ar = a - 1 + k
+        ar = first + g - 1 + k
 
         def inside(cb):
             ok = (ar >= 0) & (ar < blocks) & (cb >= ar) & (cb - ar < BAND) & (cb < blocks)
             return jnp.where(ok, 1.0, 0.0).astype(F32)
 
-        mask_s[k] = jnp.where(
-            at_left, inside(b - 1), jnp.where(at_right, inside(b + 1), inside(b))
+        bg = first + g + d
+        mask_s[new, k] = jnp.where(
+            at_left, inside(bg - 1), jnp.where(at_right, inside(bg + 1), inside(bg))
         )
 
-    uq = uq_s[...]
-    wq = wq_s[...]
-
-    def kind(i):
-        return 0 if i == 0 else (2 if i == SLABS - 1 else 1)
+    def edged(value, which, k):
+        mask = mask_s.at[which, k]
+        if k != 1:
+            return value * mask[...]
+        return jnp.concatenate(
+            [
+                value[:STEP] * mask[:STEP, :],
+                value[STEP : PLANE - STEP],
+                value[PLANE - STEP :] * mask[PLANE - STEP :, :],
+            ],
+            axis=0,
+        )
+
+    def make_map(i, r):
+        u = u_row[pl.ds(i * STEP + r, 1), :]
+        w = w_row[new, pl.ds(i * STEP + r, 1), :]
+        value = edged((u + uq_s[...]) + w * wq_s[new], new, kind(i))
+        x_s[new, i, pl.ds(r * PLANE, PLANE), :] = value.astype(BF)
 
     def make_maps(r, carry):
         for i in range(SLABS):
-            u = u_row[pl.ds(i * STEP + r, 1), :]
-            w = w_row[pl.ds(i * STEP + r, 1), :]
-            value = ((u + uq) + w * wq) * mask_s[kind(i)]
-            x_s[i, pl.ds(pl.multiple_of(r * PLANE, PLANE), PLANE), :] = value.astype(BF)
+            make_map(i, r)
         return carry
 
-    lax.fori_loop(0, STEP, make_maps, 0)
-
-    c0_s[...] = jnp.zeros_like(c0_s)
-    c1_s[...] = jnp.zeros_like(c1_s)
+    @pl.when(g == 0)
+    def _():
+        lax.fori_loop(0, STEP, make_maps, 0)
+
     bias = vec_ref[0:1, :]
     read = vec_ref[1:2, :]
+    half_read = 0.5 * read
     read_density = read * INV_SQRT_TAU
     planes = CHUNK // PLANE
 
-    def step(ch, carry):
-        r0 = ch * planes
-        at = pl.multiple_of(ch * CHUNK, CHUNK)
-        rows = pl.ds(at, CHUNK)
-        grads = []
-        for ig in range(2):
-            maps = jnp.concatenate([x_s[4 * ig + i, rows, :] for i in range(6)], axis=1)
-            v = dot(maps, wf_ref[...]) + bias
-            cdf = 0.5 * (1.0 + lax.erf(v * SQRT_HALF))
-            density = jnp.exp(-0.5 * v * v)
-            read_cdf = read * cdf
-            g = v * read_cdf
-            high = g.astype(BF)
-            low = (g - high.astype(F32)).astype(BF)
-            pred = dot(high, ones_ref[...]) + dot(low, ones_ref[...])
-            target = dot(tgt_ref[0, rows, :], place_ref[ig])
+    def tile(t):
+        a = first + t
+        b = a + d
+        reach = s_ref[blocks + a]
+        c0_s[...] = jnp.zeros_like(c0_s)
+        c1_s[...] = jnp.zeros_like(c1_s)
+
+        turned = tgt_ref[0].astype(F32).T.reshape(PAIRS, 2, STEP, TILE)
+        sides = [turned[:, jj].reshape(PLANE, TILE) for jj in range(2)]
+
+        def make_target(r):
+            for jj in range(2):
+                value = sides[jj] if r == 0 else pltpu.roll(sides[jj], TILE - r, 1)
+                tgt_s[r * PLANE : (r + 1) * PLANE, TILE * jj : TILE * (jj + 1)] = value.astype(BF)
+
+        n = ROWS // CHUNK
+        todo = [(ch, ig) for ch in range(n) for ig in range(2)]
+        vs, parts, grads = {}, {}, {}
+
+        def maps(ch, ig, begin=0, count=CHUNK):
+            rows = pl.ds(ch * CHUNK + begin, count)
+            return jnp.concatenate([x_s[old, 4 * ig + i, rows, :] for i in range(6)], axis=1)
+
+        def forward(m):
+            ch, ig = todo[m]
+            def piece(begin):
+                vs[m, begin] = dot(maps(ch, ig, begin, MPIECE), wf_ref[...])
+
+            return [functools.partial(piece, x) for x in range(0, CHUNK, MPIECE)]
+
+        def slope(m):
+            def piece(begin):
+                base = begin // MPIECE * MPIECE
+                v = vs[m, base][begin - base : begin - base + PLANE] + bias
+                x = v * SQRT_HALF
+                read_cdf = half_read * lax.erf(x) + half_read
+                value = v * read_cdf
+                high = value.astype(BF)
+                low = (value - high.astype(F32)).astype(BF)
+                parts[m, begin] = (
+                    high,
+                    low,
+                    read_cdf + (read_density * v) * jnp.exp(-(x * x)),
+                )
+
+            return [functools.partial(piece, x) for x in range(0, CHUNK, PLANE)]
+
+        def error(m):
+            ch, ig = todo[m]
             lowest = 64 * ig - TILE * d
             highest = jnp.where(b < blocks, reach + lowest, -100000)
-            dist = dist_s[rows, :]
-            keep = (dist >= lowest) & (dist <= highest)
-            err = jnp.where(keep, pred - target, 0.0) * TILE ** (-0.5)
-            grad = (err * (read_cdf + read_density * (v * density))).astype(BF)
-            grads.append(grad)
-            acc_s[...] += dot(grad, maps, (((0,), (0,)), ((), ())))
-        for k in range(SLABS // 2):
-            total = None
-            for ig in range(2):
-                slot = k - 2 * ig
-                if 0 <= slot < 3:
-                    part = dot(grads[ig], wb_ref[:, 256 * slot : 256 * (slot + 1)])
-                    total = part if total is None else total + part
-            for half in range(2):
+            out = {}
+
+            def predict(base):
+                pieces = [parts[m, base + x] for x in range(0, MPIECE, PLANE)]
+                terms = jnp.concatenate(
+                    [
+                        jnp.concatenate([x[0] for x in pieces], axis=0),
+                        jnp.concatenate([x[1] for x in pieces], axis=0),
+                        tgt_s[pl.ds(ch * CHUNK + base, MPIECE), :],
+                    ],
+                    axis=1,
+                )
+                out[base] = dot(terms, place_ref[ig])
+
+            def piece(begin):
+                base = begin // MPIECE * MPIECE
+                dist = dist_s[pl.ds(ch * CHUNK + begin, PLANE), :]
+                keep = (dist >= lowest) & (dist <= highest)
+                miss = out[base][begin - base : begin - base + PLANE]
+                err = jnp.where(keep, miss, 0.0) * TILE ** (-0.5)
+                grads[m, begin] = (err * parts[m, begin][2]).astype(BF)
+
+            todo_list = []
+            for base in range(0, CHUNK, MPIECE):
+                todo_list.append(functools.partial(predict, base))
+                if base:
+                    todo_list += [
+                        functools.partial(piece, x) for x in range(base - MPIECE, base, PLANE)
+                    ]
+            todo_list += [
+                functools.partial(piece, x) for x in range(CHUNK - MPIECE, CHUNK, PLANE)
+            ]
+            return todo_list
+
+        def grad_of(m):
+            return jnp.concatenate([grads[m, x] for x in range(0, CHUNK, PLANE)], axis=0)
+
+        def taps(m):
+            ch, ig = todo[m]
+
+            def piece(k):
+                rows = pl.ds(ch * CHUNK, CHUNK)
+                two = jnp.concatenate(
+                    [x_s[old, 4 * ig + 2 * k + i, rows, :] for i in range(2)], axis=1
+                )
+                acc_s[:, 256 * k : 256 * (k + 1)] += dot(
+                    grad_of(m), two, (((0,), (0,)), ((), ()))
+                )
+
+            return [functools.partial(piece, k) for k in range(3)]
+
+        def back(m):
+            ch, _ = todo[m]
+            totals = {}
+
+            def product(k):
+                total = None
+                for ig in range(2):
+                    slot = k - 2 * ig
+                    if 0 <= slot < 3:
+                        part = dot(grad_of(m - 1 + ig), wb_ref[:, 256 * slot : 256 * (slot + 1)])
+                        total = part if total is None else total + part
+                totals[k] = total
+
+            def piece(k, half, rr):
                 i = 2 * k + half
-                dx = total[:, 128 * half : 128 * (half + 1)].reshape(planes, PLANE, 128)
-                dx = dx * mask_s[kind(i)][None]
-                dxw = dx * wq_s[...][None]
-                for rr in range(planes):
-                    p = i * STEP + r0 + rr
-                    r0_s[p] = jnp.sum(dx[rr].reshape(PLANE // 8, 8, 128), axis=0)
-                    r1_s[p] = jnp.sum(dxw[rr].reshape(PLANE // 8, 8, 128), axis=0)
-                    c0_s[...] += dx[rr]
-                    c1_s[...] += dx[rr] * w_row[pl.ds(p, 1), :]
-        return carry
-
-    lax.fori_loop(0, ROWS // CHUNK, step, 0)
-
-    lanes = lax.broadcasted_iota(jnp.int32, (SPAN, 128), 1)
-    even = lanes // C % 2 == 0
-    row_terms = jnp.where(
-        even,
-        lane_fold(jnp.sum(r0_s[...], axis=1)),
-        lane_fold(jnp.sum(r1_s[...], axis=1)),
-    )
-    here = pl.ds(pl.multiple_of(t * TILE, TILE), SPAN)
-    row_acc[here, :] += row_terms
-
-    group = lax.broadcasted_iota(jnp.int32, (STEP, 128), 1) // C
-
-    def unwind(ref):
-        parts = []
-        for m in range(PAIRS + 1):
-            for odd in range(2):
-                value = jnp.zeros((STEP, 128), F32)
-                if m < PAIRS:
-                    value = jnp.where(group == odd, ref[m * STEP : (m + 1) * STEP, :], value)
-                if m > 0:
-                    value = jnp.where(group == 2 + odd, ref[(m - 1) * STEP : m * STEP, :], value)
-                parts.append(value)
-        return lane_fold(jnp.concatenate(parts, axis=0))
-
-    col_acc[here, :] += jnp.where(even, unwind(c0_s), unwind(c1_s))
-
-    @pl.when(t == tiles - 1)
+                p = i * STEP + ch * planes + rr
+                dx = totals[k][rr * PLANE : (rr + 1) * PLANE, 128 * half : 128 * (half + 1)]
+                dx = edged(dx, old, kind(i))
+                c0_s[...] += dx
+                c1_s[...] += dx * w_row[old, p : p + 1, :]
+                r0_s[p] = jnp.sum(dx.reshape(PLANE // 8, 8, 128), axis=0)
+                r1_s[p] = jnp.sum((dx * wq_s[old]).reshape(PLANE // 8, 8, 128), axis=0)
+
+            out = []
+            for k in range(SLABS // 2):
+                out.append(functools.partial(product, k))
+                if k:
+                    out += [
+                        functools.partial(piece, k - 1, half, rr)
+                        for half in range(2)
+                        for rr in range(planes)
+                    ]
+            out += [
+                functools.partial(piece, SLABS // 2 - 1, half, rr)
+                for half in range(2)
+                for rr in range(planes)
+            ]
+            return out
+
+        targets = [functools.partial(make_target, r) for r in range(STEP)]
+        fresh = [functools.partial(make_map, i, r) for r in range(STEP) for i in range(SLABS)]
+        units = len(todo)
+        steps = units + 3
+        for m in range(steps):
+            share = fresh[len(fresh) * m // steps : len(fresh) * (m + 1) // steps]
+            tgt_now = targets[STEP * m // 2 : STEP * (m + 1) // 2] if m < 2 else []
+            weave(
+                forward(m) if m < units else [],
+                slope(m - 1) if 0 <= m - 1 < units else [],
+                error(m - 2) if 0 <= m - 2 < units else [],
+                taps(m - 3) if m >= 3 else [],
+                back(m - 3) if m >= 3 and (m - 3) % 2 == 1 else [],
+                share,
+                tgt_now,
+            )
+
+        lanes = lax.broadcasted_iota(jnp.int32, (SPAN, 128), 1)
+        even = lanes // C % 2 == 0
+        row_terms = jnp.where(
+            even,
+            lane_fold(jnp.sum(r0_s[...], axis=1)),
+            lane_fold(jnp.sum(r1_s[...], axis=1)),
+        )
+        here = pl.ds(pl.multiple_of(t * TILE, TILE), SPAN)
+        row_acc[here, :] += row_terms
+
+        group = lax.broadcasted_iota(jnp.int32, (STEP, 128), 1) // C
+
+        def unwind(ref):
+            pieces = []
+            for m in range(PAIRS + 1):
+                for odd in range(2):
+                    value = jnp.zeros((STEP, 128), F32)
+                    if m < PAIRS:
+                        value = jnp.where(group == odd, ref[m * STEP : (m + 1) * STEP, :], value)
+                    if m > 0:
+                        value = jnp.where(
+                            group == 2 + odd, ref[(m - 1) * STEP : m * STEP, :], value
+                        )
+                    pieces.append(value)
+            return lane_fold(jnp.concatenate(pieces, axis=0))
+
+        col_acc[here, :] += jnp.where(even, unwind(c0_s), unwind(c1_s))
+
+    @pl.when(g > 0)
+    def _():
+        tile(g - 1)
+
+    @pl.when(g == tiles)
     def _():
         grads_ref[...] = jnp.zeros_like(grads_ref)
-        first = s_ref[2 * blocks] * tiles
         low_half = lax.broadcasted_iota(jnp.int32, (32, 128), 1) < 64
 
         def put(acc_ref, base, k, begin, count):
@@ -268,18 +408,30 @@
             taps_ref[ty] = total[:C] + pltpu.roll(total[C:], 96, 1)
 
 
-def run_tiles(scalars, code_chunks, tgt, wf, wb, vec, blocks, tiles):
+def run_tiles(scalars, code_chunks, targets, wf, wb, vec, blocks, tiles):
     lane = jnp.arange(256, dtype=jnp.int32)
     source = lane // 128 * C + lane % C
     depth = jnp.arange(128, dtype=jnp.int32)
     spread = jnp.stack(
         [depth[:, None] == source[None, :], depth[:, None] == 64 + source[None, :]]
     ).astype(BF)
-    ones = (lane[:, None] // C == lane[None, :] // C).astype(BF)
-    sixteen = jnp.arange(16, dtype=jnp.int32)
+    ones = lane[:, None] // C == lane[None, :] // C
     place = jnp.stack(
-        [sixteen[:, None] == 8 * ig + lane[None, :] // C for ig in range(2)]
-    ).astype(BF)
+        [
+            jnp.concatenate(
+                [ones.astype(BF), ones.astype(BF)]
+                + [
+                    -(
+                        (depth[:, None] == 16 * (4 * ig + lane[None, :] // 64))
+                        & (lane[None, :] // C % 2 == jj)
+                    ).astype(BF)
+                    for jj in range(2)
+                ],
+                axis=0,
+            )
+            for ig in range(2)
+        ]
+    )
 
     def chunk_spec(offset, column, edge):
         def index(t, s):
@@ -301,7 +453,7 @@
 
     grid_spec = pltpu.PrefetchScalarGridSpec(
         num_scalar_prefetch=1,
-        grid=(tiles,),
+        grid=(tiles + 1,),
         in_specs=[
             chunk_spec(-1, False, -1),
             chunk_spec(0, False, 0),
@@ -309,11 +461,10 @@
             chunk_spec(-1, True, -1),
             chunk_spec(0, True, 0),
             chunk_spec(1, True, 1),
-            pl.BlockSpec((1, ROWS, 16), lambda t, s: (t, 0, 0)),
+            pl.BlockSpec((1, TILE, TILE), lambda t, s: (jnp.maximum(t - 1, 0), 0, 0)),
             whole(wf),
             whole(wb),
             whole(spread),
-            whole(ones),
             whole(place),
             whole(vec),
         ],
@@ -323,12 +474,13 @@
         ],
         scratch_shapes=[
             pltpu.VMEM((SPAN, 128), F32),
-            pltpu.VMEM((SPAN, 128), F32),
+            pltpu.VMEM((2, SPAN, 128), F32),
             pltpu.VMEM((PLANE, 128), F32),
-            pltpu.VMEM((PLANE, 128), F32),
-            pltpu.VMEM((3, PLANE, 128), F32),
+            pltpu.VMEM((2, PLANE, 128), F32),
+            pltpu.VMEM((2, 3, PLANE, 128), F32),
             pltpu.VMEM((ROWS, 256), jnp.int32),
-            pltpu.VMEM((SLABS, ROWS, 128), BF),
+            pltpu.VMEM((ROWS, 256), BF),
+            pltpu.VMEM((2, SLABS, ROWS, 128), BF),
             pltpu.VMEM((SPAN, 8, 128), F32),
             pltpu.VMEM((SPAN, 8, 128), F32),
             pltpu.VMEM((PLANE, 128), F32),
@@ -356,11 +508,10 @@
         code_chunks,
         code_chunks,
         code_chunks,
-        tgt,
+        targets,
         wf,
         wb,
         spread,
-        ones,
         place,
         vec,
     )
@@ -395,11 +546,6 @@
             jnp.stack([lax.axis_index("row"), lax.axis_index("diag")]).astype(jnp.int32),
         ]
     )
-    tgt = (
-        targets.reshape(tiles, GROUPS, STEP, PAIRS, 2, STEP)
-        .transpose(0, 2, 3, 5, 1, 4)
-        .reshape(tiles, ROWS, 2 * GROUPS)
-    )
     taps = convolution_weight.reshape(3, 3, C, C).transpose(0, 1, 3, 2)
     wf = jnp.stack(
         [
@@ -411,7 +557,7 @@
     ).reshape(768, 256)
     wb = wf.T
     vec = jnp.stack([jnp.tile(convolution_bias, 8), jnp.tile(readout, 8)])
-    grads, tap_sums = run_tiles(scalars, code_chunks, tgt, wf, wb, vec, blocks, tiles)
+    grads, tap_sums = run_tiles(scalars, code_chunks, targets, wf, wb, vec, blocks, tiles)
     tap_flat = (
         tap_sums[:, :, : 3 * C].reshape(3, C, 3, C).transpose(0, 2, 1, 3).reshape(2 * blocks, -1)
         / blocks

time: 132 us -> 109 us (0.83)
  Pallas kernels: 66.8 us -> 46.3 us
  local copies, waits for them, and re-layouts: 17.9 us -> 5.03 us
  waiting for transfers between devices: 3.54 us -> 16.2 us
  blocking collectives: 28.1 us -> 26.4 us
    pallas_call x1, Pallas kernels: 66.8 us -> 46.3 us  [run_tiles(): pl.pallas_call(functools.partial(tile_kernel, blocks, tiles), grid_spec=g...]
    reshape x4 -> x0, local copies, waits for them, and re-layouts: 12.9 us -> none  [the longest x2 6.46 us: per_device(): tgt = targets.reshape(tiles, GROUPS, STEP, PAIRS, 2, STEP).transpose(0, 2...]
    all_to_all x1, waiting for transfers between devices: 3.54 us -> 16.2 us  [per_device(): lax.all_to_all(jnp.broadcast_to(packed[None], (2 * blocks, 32, 128)), axe...]
    all_to_all x1, blocking collectives: 28.1 us -> 26.4 us  [per_device(): received = lax.all_to_all(terms, axes, 0, 0, tiled=True)]
  transfers between devices with their start and end apart: 1 -> 1, of which waited for: 1 -> 1; matrix products, arithmetic and copies ran while one was open for 12% -> 3% of each run, Pallas kernels for 0% -> 0%
where the time goes in v2:
time: 109 us
  Pallas kernels  46.3 us (42%)
  blocking collectives  26.4 us (24%)
  waiting for transfers between devices  16.2 us (15%)
  starting transfers between devices  11.1 us (10%)
  local copies, waits for them, and re-layouts  5.03 us (5%)
  other arithmetic  1.94 us (2%)
    pallas_call x1, Pallas kernels, run_tiles(): pl.pallas_call(functools.partial(tile_kernel, blocks, tiles), grid_spec=g...  46.3 us
    all_to_all x1, blocking collectives, per_device(): received = lax.all_to_all(terms, axes, 0, 0, tiled=True)  26.4 us
    all_to_all x1, waiting for transfers between devices, per_device(): lax.all_to_all(jnp.broadcast_to(packed[None], (2 * blocks, 32, 128)), axe...  16.2 us
    all_to_all x1, starting transfers between devices, per_device(): lax.all_to_all(jnp.broadcast_to(packed[None], (2 * blocks, 32, 128)), axe...  11.1 us
  transfers between devices with their start and end apart: 1, of which 1 were waited for; matrix products, arithmetic and copies ran while one was open for 3% of the time, Pallas kernels for 0%

profile of v2, /device:TPU:0, one launch (start us, length us, event | category | flops | bytes accessed | tf_op | source)
XLA Modules:
  0.0 108.8 jit_solution(14934875194810833568)
XLA Ops:
  0.6 0.0 copy-start
  0.6 0.7 copy-done
  1.4 0.9 convolution_convert_fusion
  2.3 0.1 pad_maximum_fusion.4
  2.4 0.0 copy-start.2
  2.4 1.1 %broadcast_in_dim.16 = bf16[128,32,128]{2,1,0:T(8,128)(2,1)} broadcast(bf16[32,128]{1,0:T(8,128)(2,1)S(1)} %pad_maximum_fusion.4), dimensions={1,2} | broadcast | bytes 1056768 | tf_op jit(solution)/shard_map/broadcast_in_dim | solution.py:536
  3.5 11.1 %all-to-all-start = ((bf16[128,32,128]{2,1,0:T(8,128)(2,1)}), bf16[128,32,128]{2,1,0:T(8,128)(2,1)S(1)}, u32[]{:S(2)}, u32[]{:S(2)}) async-start(bf16[128,32,128]{2,1,0:T(8,128)(2,1)} %broadcast_in_dim.16), calls=%async_computation | async-start | bytes 2097152 | tf_op jit(solution)/shard_map/all_to_all | solution.py:535
  14.7 0.0 copy-done.2
  14.7 0.1 copy.20
  14.8 0.1 bitcast_dynamic-update-slice_fusion.7
  14.8 0.1 bitcast_dynamic-update-slice_fusion.6
  15.0 0.1 bitcast_dynamic-update-slice_fusion.5
  15.1 0.1 bitcast_dynamic-update-slice_fusion.4
  15.2 0.1 bitcast_dynamic-update-slice_fusion.3
  15.3 0.1 bitcast_dynamic-update-slice_fusion.2
  15.4 0.1 bitcast_dynamic-update-slice_fusion.1
  15.5 0.0 copy-start.6
  15.5 0.0 copy-start.3
  15.5 0.0 copy-start.4
  15.5 0.0 copy-start.5
  15.5 0.1 bitcast_dynamic-update-slice_fusion
  15.6 1.0 reshape.249
  16.7 0.2 copy.16.wf_ref
  16.8 0.0 copy-done.6
  16.8 0.1 select_reduce_fusion
  16.9 0.0 copy-done.3
  17.0 0.1 stack_tile.6
  17.0 0.0 copy-done.4
  17.0 0.1 stack_tile.7
  17.1 0.0 copy-done.5
  17.1 0.1 pad_add_fusion.s_ref
  17.3 0.0 copy-start.1
  17.3 0.1 compare_convert_fusion
  17.4 0.1 fusion.9
  17.5 0.1 maximum_bitcast_fusion
  17.6 0.1 pad_maximum_fusion.1.place_ref
  17.6 16.2 %all-to-all-done.row_prev.row_here.row_next.col_prev.col_here.col_next = bf16[128,32,128]{2,1,0:T(8,128)(2,1)S(1)} async-done(((bf16[128,32,128]{2,1,0:T(8,128)(2,1)}), bf16[128,32,128]{2,1,0:T(8,128)(2,1)S(1)}, u32[]{:S(2)}, u32[]{:S(2)}) %all-to-all-start) | async-done | bytes 1048608 | tf_op jit(solution)/shard_map/all_to_all | solution.py:535
  33.8 0.0 copy-done.1
  33.8 46.3 %shard_map.95 = (f32[128,32,128]{2,1,0:T(8,128)S(1)}, f32[3,32,128]{2,1,0:T(8,128)S(1)}) custom-call(s32[130]{0:T(256)S(1)} %pad_add_fusion.s_ref, bf16[128,32,128]{2,1,0:T(8,128)(2,1)S(1)} %all-to-all-done.row_prev.row_here.row_next.col_prev.col_here.col_next, bf16[128,32,128]{2,1,0:T(8,128)(2,1)S(1)} %all-to-all-done.row_prev.row_here.row_next.col_prev.col_here.col_next, ...), custom_call_target="tpu_custom_call" | custom-call | tf_op jit(solution)/shard_map/pallas_call | solution.py:493
  80.2 0.2 convert_element_type.65
  80.4 0.1 div.82
  80.5 0.1 div.84
  80.8 0.2 pad_maximum_fusion
  81.0 26.4 %all_to_all.10 = bf16[128,40,128]{2,1,0:T(8,128)(2,1)S(1)} all-to-all(bf16[128,40,128]{2,1,0:T(8,128)(2,1)S(1)} %pad_maximum_fusion), channel_id=1, replica_groups=mesh['row'=8,'diag'=16] {'row','diag'}, dimensions={0} | all-to-all | bytes 2621440 | tf_op jit(solution)/shard_map/all_to_all | solution.py:568
  107.3 0.2 convert_reduce_fusion
  107.6 0.1 fusion.18
  107.6 0.5 slice_bitcast_fusion
  108.2 0.6 pad_maximum_fusion.3
  (15 shorter events, 0.2 us)
Async XLA Ops:
  0.6 0.8 copy-start
  2.4 12.3 %copy-start.2 = (bf16[9,32,32]{2,1,0:T(8,128)(2,1)S(1)}, bf16[9,32,32]{2,1,0:T(8,128)(2,1)}, u32[]{:S(2)}) copy-start(bf16[9,32,32]{2,1,0:T(8,128)(2,1)} %param.10) | copy-start | bytes 55300
  3.5 30.3 %all-to-all-start = ((bf16[128,32,128]{2,1,0:T(8,128)(2,1)}), bf16[128,32,128]{2,1,0:T(8,128)(2,1)S(1)}, u32[]{:S(2)}, u32[]{:S(2)}) async-start(bf16[128,32,128]{2,1,0:T(8,128)(2,1)} %broadcast_in_dim.16), calls=%async_computation | async-start | bytes 2097152 | tf_op jit(solution)/shard_map/all_to_all | solution.py:535
  15.5 1.4 %copy-start.6 = (s32[64]{0:T(128)S(1)}, s32[64]{0:T(128)}, u32[]{:S(2)}) copy-start(s32[64]{0:T(128)} %param.14) | copy-start | bytes 772
  15.5 1.4 %copy-start.3 = (f32[32]{0:T(128)S(1)}, f32[32]{0:T(128)}, u32[]{:S(2)}) copy-start(f32[32]{0:T(128)} %param.11) | copy-start | bytes 388
  15.5 1.5 %copy-start.4 = (f32[32]{0:T(128)S(1)}, f32[32]{0:T(128)}, u32[]{:S(2)}) copy-start(f32[32]{0:T(128)} %param.12) | copy-start | bytes 388
  15.5 1.6 %copy-start.5 = (s32[64]{0:T(128)S(1)}, s32[64]{0:T(128)}, u32[]{:S(2)}) copy-start(s32[64]{0:T(128)} %param.15) | copy-start | bytes 772
  17.3 16.5 %copy-start.1 = (bf16[8,128,128]{2,1,0:T(8,128)(2,1)S(1)}, bf16[8,128,128]{2,1,0:T(8,128)(2,1)}, u32[]{:S(2)}) copy-start(bf16[8,128,128]{2,1,0:T(8,128)(2,1)} %tgt_ref.1) | copy-start | bytes 786436

commit v3 on v2

--- a/solution.py
+++ b/solution.py
@@ -18,8 +18,10 @@
 ROWS = STEP * PLANE
 CHUNK = 512
 MPIECE = 512
+GROUP = 8
 
 SQRT_HALF = 0.7071067811865476
+HALF_LOG2E = -0.7213475204444817
 INV_SQRT_TAU = 0.3989422804014327
 BF = jnp.bfloat16
 F32 = jnp.float32
@@ -27,6 +29,22 @@
 
 def dot(a, b, dims=(((1,), (0,)), ((), ()))):
     return lax.dot_general(a, b, dims, preferred_element_type=F32)
+
+
+def rows_of_sums(parts):
+    x = [parts[n] for n in (3, 7, 1, 5, 2, 6, 0, 4)]
+    s = lax.broadcasted_iota(jnp.int32, (8, 128), 0)
+    upper, second, odd = s < 4, s // 2 % 2 == 1, s % 2 == 1
+    x = [
+        jnp.where(upper, p, q) + pltpu.roll(jnp.where(upper, q, p), 4, 0)
+        for p, q in zip(x[0::2], x[1::2])
+    ]
+    x = [
+        jnp.where(second, p + pltpu.roll(p, 2, 0), q + pltpu.roll(q, 6, 0))
+        for p, q in zip(x[0::2], x[1::2])
+    ]
+    p, q = x
+    return jnp.where(odd, p + pltpu.roll(p, 1, 0), q + pltpu.roll(q, 7, 0))
 
 
 def lane_fold(x):
@@ -58,6 +76,7 @@
     wb_ref,
     spread_ref,
     place_ref,
+    pick_ref,
     vec_ref,
     grads_ref,
     taps_ref,
@@ -65,12 +84,11 @@
     w_row,
     uq_s,
     wq_s,
+    wq_plain,
     mask_s,
     dist_s,
     tgt_s,
     x_s,
-    r0_s,
-    r1_s,
     c0_s,
     c1_s,
     acc_s,
@@ -95,7 +113,9 @@
         s = line % STEP
         ii = lane // 64
         jj = (lane // 32) % 2
-        dist_s[...] = 32 * jp + s - r + 16 * (jj - ii)
+        for ig in range(2):
+            dist = TILE * d - 64 * ig + 32 * jp + s - r + 16 * (jj - ii)
+            dist_s[ig] = jnp.where(dist >= 0, dist, 1 << 20).astype(F32)
 
     def codes(prev, here, after):
         left, right = spread_ref[0], spread_ref[1]
@@ -114,32 +134,37 @@
     def kind(i):
         return 0 if i == 0 else (2 if i == SLABS - 1 else 1)
 
-    row_codes = codes(row_prev, row_here, row_next)
-    u_row[...] = row_codes[:, :128]
-    w_row[new] = row_codes[:, 128:]
-    col_codes = codes(col_prev, col_here, col_next).reshape(SLABS, STEP, 256)
-    group = lax.broadcasted_iota(jnp.int32, (STEP, 256), 1) // C % 4
-    for jp in range(PAIRS):
-        window = col_codes[2 * jp]
-        for m in range(1, 4):
-            window = jnp.where(group == m, col_codes[2 * jp + m], window)
-        uq_s[jp * STEP : (jp + 1) * STEP, :] = window[:, :128]
-        wq_s[new, jp * STEP : (jp + 1) * STEP, :] = window[:, 128:]
-    line = lax.broadcasted_iota(jnp.int32, (PLANE, 128), 0)
-    lane = lax.broadcasted_iota(jnp.int32, (PLANE, 128), 1)
-    at_left = (line < STEP) & (lane < C)
-    at_right = (line >= PLANE - STEP) & (lane >= 3 * C)
-    for k in range(3):
-        ar = first + g - 1 + k
-
-        def inside(cb):
-            ok = (ar >= 0) & (ar < blocks) & (cb >= ar) & (cb - ar < BAND) & (cb < blocks)
-            return jnp.where(ok, 1.0, 0.0).astype(F32)
-
-        bg = first + g + d
-        mask_s[new, k] = jnp.where(
-            at_left, inside(bg - 1), jnp.where(at_right, inside(bg + 1), inside(bg))
-        )
+    def prepare():
+        row_codes = codes(row_prev, row_here, row_next)
+        u_row[...] = row_codes[:, :128]
+        w_row[new] = row_codes[:, 128:]
+        col_codes = codes(col_prev, col_here, col_next).reshape(SLABS, STEP, 256)
+        group = lax.broadcasted_iota(jnp.int32, (STEP, 256), 1) // C % 4
+        for jp in range(PAIRS):
+            window = col_codes[2 * jp]
+            for m in range(1, 4):
+                window = jnp.where(group == m, col_codes[2 * jp + m], window)
+            uq_s[jp * STEP : (jp + 1) * STEP, :] = window[:, :128]
+            wq_s[new, 1, jp * STEP : (jp + 1) * STEP, :] = window[:, 128:]
+        line = lax.broadcasted_iota(jnp.int32, (PLANE, 128), 0)
+        lane = lax.broadcasted_iota(jnp.int32, (PLANE, 128), 1)
+        at_left = (line < STEP) & (lane < C)
+        at_right = (line >= PLANE - STEP) & (lane >= 3 * C)
+        for k in range(3):
+            ar = first + g - 1 + k
+
+            def inside(cb):
+                ok = (ar >= 0) & (ar < blocks) & (cb >= ar) & (cb - ar < BAND) & (cb < blocks)
+                return jnp.where(ok, 1.0, 0.0).astype(F32)
+
+            bg = first + g + d
+            mask_s[new, k] = jnp.where(
+                at_left, inside(bg - 1), jnp.where(at_right, inside(bg + 1), inside(bg))
+            )
+        plain_w = wq_s[new, 1]
+        wq_plain[...] = plain_w
+        for k in range(3):
+            wq_s[new, k] = plain_w * mask_s[new, k]
 
     def edged(value, which, k):
         mask = mask_s.at[which, k]
@@ -157,7 +182,7 @@
     def make_map(i, r):
         u = u_row[pl.ds(i * STEP + r, 1), :]
         w = w_row[new, pl.ds(i * STEP + r, 1), :]
-        value = edged((u + uq_s[...]) + w * wq_s[new], new, kind(i))
+        value = edged((u + uq_s[...]) + w * wq_plain[...], new, kind(i))
         x_s[new, i, pl.ds(r * PLANE, PLANE), :] = value.astype(BF)
 
     def make_maps(r, carry):
@@ -167,6 +192,7 @@
 
     @pl.when(g == 0)
     def _():
+        prepare()
         lax.fori_loop(0, STEP, make_maps, 0)
 
     bias = vec_ref[0:1, :]
@@ -176,6 +202,7 @@
     planes = CHUNK // PLANE
 
     def tile(t):
+        prepare()
         a = first + t
         b = a + d
         reach = s_ref[blocks + a]
@@ -192,23 +219,41 @@
 
         n = ROWS // CHUNK
         todo = [(ch, ig) for ch in range(n) for ig in range(2)]
-        vs, parts, grads = {}, {}, {}
-
-        def maps(ch, ig, begin=0, count=CHUNK):
-            rows = pl.ds(ch * CHUNK + begin, count)
-            return jnp.concatenate([x_s[old, 4 * ig + i, rows, :] for i in range(6)], axis=1)
+        products, parts, grads, flips, sums = {}, {}, {}, {}, {}
+
+        def pair(ch, k):
+            rows = pl.ds(ch * CHUNK, CHUNK)
+            return jnp.concatenate([x_s[old, 2 * k + i, rows, :] for i in range(2)], axis=1)
 
         def forward(m):
             ch, ig = todo[m]
-            def piece(begin):
-                vs[m, begin] = dot(maps(ch, ig, begin, MPIECE), wf_ref[...])
-
-            return [functools.partial(piece, x) for x in range(0, CHUNK, MPIECE)]
+
+            def first_pair():
+                products[ch, 0] = dot(pair(ch, 0), wf_ref[:, 128:])
+
+            def piece(k):
+                products[ch, k] = dot(pair(ch, k), wf_ref[...])
+
+            def last_pair():
+                products[ch, 4] = dot(pair(ch, 4), wf_ref[:, :128])
+
+            if ig == 0:
+                return [first_pair] + [functools.partial(piece, k) for k in (1, 2)]
+            return [functools.partial(piece, 3), last_pair]
+
+        def summed(m, begin):
+            ch, ig = todo[m]
+            rows = slice(begin, begin + PLANE)
+            if ig == 0:
+                left, right = products[ch, 0][rows], products[ch, 2][rows, :128]
+            else:
+                left, right = products[ch, 2][rows, 128:], products[ch, 4][rows]
+            middle = products[ch, 2 * ig + 1][rows]
+            return jnp.concatenate([middle[:, :128] + left, middle[:, 128:] + right], axis=1)
 
         def slope(m):
             def piece(begin):
-                base = begin // MPIECE * MPIECE
-                v = vs[m, base][begin - base : begin - base + PLANE] + bias
+                v = summed(m, begin) + bias
                 x = v * SQRT_HALF
                 read_cdf = half_read * lax.erf(x) + half_read
                 value = v * read_cdf
@@ -217,15 +262,14 @@
                 parts[m, begin] = (
                     high,
                     low,
-                    read_cdf + (read_density * v) * jnp.exp(-(x * x)),
+                    read_cdf + (read_density * v) * jnp.exp2(v * (v * HALF_LOG2E)),
                 )
 
             return [functools.partial(piece, x) for x in range(0, CHUNK, PLANE)]
 
         def error(m):
             ch, ig = todo[m]
-            lowest = 64 * ig - TILE * d
-            highest = jnp.where(b < blocks, reach + lowest, -100000)
+            farthest = jnp.where(b < blocks, reach, -1).astype(F32)
             out = {}
 
             def predict(base):
@@ -242,8 +286,7 @@
 
             def piece(begin):
                 base = begin // MPIECE * MPIECE
-                dist = dist_s[pl.ds(ch * CHUNK + begin, PLANE), :]
-                keep = (dist >= lowest) & (dist <= highest)
+                keep = dist_s[ig, pl.ds(ch * CHUNK + begin, PLANE), :] <= farthest
                 miss = out[base][begin - base : begin - base + PLANE]
                 err = jnp.where(keep, miss, 0.0) * TILE ** (-0.5)
                 grads[m, begin] = (err * parts[m, begin][2]).astype(BF)
@@ -260,60 +303,94 @@
             ]
             return todo_list
 
-        def grad_of(m):
-            return jnp.concatenate([grads[m, x] for x in range(0, CHUNK, PLANE)], axis=0)
+        def joined(m):
+            whole = jnp.concatenate([grads[m, x] for x in range(0, CHUNK, PLANE)], axis=0)
+            flips[m] = (whole, whole.T)
+
+        def plain(m):
+            ch, ig = todo[m]
+            part = dot(pick_ref[:, pl.ds(ch * CHUNK, CHUNK)], flips[m][0])
+            sums[ig] = part if ch == 0 else sums[ig] + part
+
+        def plain_back():
+            zero = jnp.zeros((2 * PLANE, 128), F32)
+            four = [sums[0][:, :128], sums[0][:, 128:], sums[1][:, :128], sums[1][:, 128:]]
+            four = [zero] + four + [zero]
+            middle = None
+            for k in range(SLABS // 2):
+                both = jnp.concatenate([four[k], four[k + 1]], axis=1)
+                high = both.astype(BF)
+                low = (both - high.astype(F32)).astype(BF)
+                out = dot(high, wb_ref[...]) + dot(low, wb_ref[...])
+                for half in range(2):
+                    i = 2 * k + half
+                    value = out[:, 128 * half : 128 * (half + 1)]
+                    rows = value[:PLANE].reshape(PAIRS, STEP, 128)
+                    mask = mask_s.at[old, kind(i)]
+                    total = rows[0] * mask[0:1, :] + rows[PAIRS - 1] * mask[PLANE - 1 : PLANE, :]
+                    for jp in range(1, PAIRS - 1):
+                        total = total + rows[jp] * mask[STEP : STEP + 1, :]
+                    here = pl.ds(pl.multiple_of(t * TILE, TILE) + i * STEP, STEP)
+                    row_acc[0, here, :] += total
+                    if kind(i) == 1:
+                        middle = value[PLANE:] if middle is None else middle + value[PLANE:]
+                    else:
+                        c0_s[...] += value[PLANE:] * mask[...]
+            c0_s[...] += middle * mask_s[old, 1]
+
+        def sides_of(m, which):
+            ch, ig = todo[m]
+            axis = 1 - which
+            take = lambda n, h: lax.slice_in_dim(flips[n][which], 128 * h, 128 * h + 128, axis=axis)
+            if ig == 0:
+                return [(0, take(m, 0), slice(128, 256)), (1, flips[m][which], slice(0, 256))]
+            return [
+                (2, jnp.concatenate([take(m - 1, 1), take(m, 0)], axis=axis), slice(0, 256)),
+                (3, flips[m][which], slice(0, 256)),
+                (4, take(m, 1), slice(0, 128)),
+            ]
 
         def taps(m):
             ch, ig = todo[m]
 
-            def piece(k):
-                rows = pl.ds(ch * CHUNK, CHUNK)
-                two = jnp.concatenate(
-                    [x_s[old, 4 * ig + 2 * k + i, rows, :] for i in range(2)], axis=1
-                )
-                acc_s[:, 256 * k : 256 * (k + 1)] += dot(
-                    grad_of(m), two, (((0,), (0,)), ((), ()))
-                )
-
-            return [functools.partial(piece, k) for k in range(3)]
+            def piece(n):
+                k, lhs, where = sides_of(m, 1)[n]
+                acc_s[where, :] += dot(lhs, pair(ch, k))
+
+            return [functools.partial(piece, n) for n in range(2 + ig)]
 
         def back(m):
-            ch, _ = todo[m]
+            ch, ig = todo[m]
             totals = {}
 
-            def product(k):
-                total = None
-                for ig in range(2):
-                    slot = k - 2 * ig
-                    if 0 <= slot < 3:
-                        part = dot(grad_of(m - 1 + ig), wb_ref[:, 256 * slot : 256 * (slot + 1)])
-                        total = part if total is None else total + part
-                totals[k] = total
-
-            def piece(k, half, rr):
+            def product(n):
+                k, lhs, where = sides_of(m, 0)[n]
+                totals[k] = dot(lhs, wb_ref[where, :])
+
+            def piece(k, half, begin):
                 i = 2 * k + half
-                p = i * STEP + ch * planes + rr
-                dx = totals[k][rr * PLANE : (rr + 1) * PLANE, 128 * half : 128 * (half + 1)]
-                dx = edged(dx, old, kind(i))
-                c0_s[...] += dx
-                c1_s[...] += dx * w_row[old, p : p + 1, :]
-                r0_s[p] = jnp.sum(dx.reshape(PLANE // 8, 8, 128), axis=0)
-                r1_s[p] = jnp.sum((dx * wq_s[old]).reshape(PLANE // 8, 8, 128), axis=0)
+                c1 = c1_s[kind(i)]
+                wq = wq_s[old, kind(i)]
+                r1 = []
+                for rr in range(begin, begin + GROUP):
+                    p = i * STEP + ch * planes + rr
+                    dx = totals[k][rr * PLANE : (rr + 1) * PLANE, 128 * half : 128 * (half + 1)]
+                    c1 = c1 + dx * w_row[old, p : p + 1, :]
+                    r1.append(jnp.sum((dx * wq).reshape(PLANE // 8, 8, 128), axis=0))
+                c1_s[kind(i)] = c1
+                rows = pl.ds(pl.multiple_of(t * TILE, TILE) + i * STEP + ch * planes + begin, 8)
+                row_acc[1, rows, :] += rows_of_sums(r1)
 
             out = []
-            for k in range(SLABS // 2):
-                out.append(functools.partial(product, k))
-                if k:
-                    out += [
-                        functools.partial(piece, k - 1, half, rr)
-                        for half in range(2)
-                        for rr in range(planes)
-                    ]
-            out += [
-                functools.partial(piece, SLABS // 2 - 1, half, rr)
-                for half in range(2)
-                for rr in range(planes)
-            ]
+            for n in range(2 + ig):
+                out.append(functools.partial(product, n))
+            for n in range(2 + ig):
+                k = n + 2 * ig
+                out += [
+                    functools.partial(piece, k, half, x)
+                    for half in range(2)
+                    for x in range(0, planes, GROUP)
+                ]
             return out
 
         targets = [functools.partial(make_target, r) for r in range(STEP)]
@@ -327,22 +404,16 @@
                 forward(m) if m < units else [],
                 slope(m - 1) if 0 <= m - 1 < units else [],
                 error(m - 2) if 0 <= m - 2 < units else [],
-                taps(m - 3) if m >= 3 else [],
-                back(m - 3) if m >= 3 and (m - 3) % 2 == 1 else [],
+                [functools.partial(joined, m - 3), functools.partial(plain, m - 3)]
+                + taps(m - 3)
+                + back(m - 3)
+                if m >= 3
+                else [],
                 share,
                 tgt_now,
             )
 
-        lanes = lax.broadcasted_iota(jnp.int32, (SPAN, 128), 1)
-        even = lanes // C % 2 == 0
-        row_terms = jnp.where(
-            even,
-            lane_fold(jnp.sum(r0_s[...], axis=1)),
-            lane_fold(jnp.sum(r1_s[...], axis=1)),
-        )
         here = pl.ds(pl.multiple_of(t * TILE, TILE), SPAN)
-        row_acc[here, :] += row_terms
-
         group = lax.broadcasted_iota(jnp.int32, (STEP, 128), 1) // C
 
         def unwind(ref):
@@ -357,9 +428,14 @@
                             group == 2 + odd, ref[(m - 1) * STEP : m * STEP, :], value
                         )
                     pieces.append(value)
-            return lane_fold(jnp.concatenate(pieces, axis=0))
-
-        col_acc[here, :] += jnp.where(even, unwind(c0_s), unwind(c1_s))
+            return jnp.concatenate(pieces, axis=0)
+
+        plain_back()
+        c1_s[0] = (
+            c1_s[0] * mask_s[old, 0] + c1_s[1] * mask_s[old, 1] + c1_s[2] * mask_s[old, 2]
+        )
+        col_acc[0, here, :] += unwind(c0_s)
+        col_acc[1, here, :] += unwind(c1_s.at[0])
 
     @pl.when(g > 0)
     def _():
@@ -369,6 +445,10 @@
     def _():
         grads_ref[...] = jnp.zeros_like(grads_ref)
         low_half = lax.broadcasted_iota(jnp.int32, (32, 128), 1) < 64
+        even = lax.broadcasted_iota(jnp.int32, row_acc.shape[1:], 1) // C % 2 == 0
+        for acc_ref in (row_acc, col_acc):
+            acc_ref[0] = jnp.where(even, lane_fold(acc_ref[0]), lane_fold(acc_ref[1]))
+
 
         def put(acc_ref, base, k, begin, count):
             n = base + k
@@ -377,8 +457,8 @@
             def _():
                 slot = s_ref[n]
                 for h in range(2):
-                    top = acc_ref[pl.ds(begin + 64 * h, 32), :]
-                    bottom = acc_ref[pl.ds(begin + 64 * h + 32, 32), :]
+                    top = acc_ref[0, pl.ds(begin + 64 * h, 32), :]
+                    bottom = acc_ref[0, pl.ds(begin + 64 * h + 32, 32), :]
                     grads_ref[2 * slot + h] += jnp.where(low_half, top, bottom)
 
         for acc_ref, base in ((row_acc, first), (col_acc, first + d)):
@@ -389,22 +469,21 @@
             def _():
                 slot = s_ref[jnp.clip(base - 1, 0, blocks - 1)]
                 grads_ref[2 * slot + 1, pl.ds(16, 16), :] += jnp.where(
-                    low_half[:16], 0.0, acc_ref[0:STEP, :]
+                    low_half[:16], 0.0, acc_ref[0, 0:STEP, :]
                 )
 
             @pl.when(base + tiles < blocks)
             def _():
                 slot = s_ref[jnp.minimum(base + tiles, blocks - 1)]
                 grads_ref[2 * slot, pl.ds(0, 16), :] += jnp.where(
-                    low_half[:16], acc_ref[STEP + tiles * TILE : 2 * STEP + tiles * TILE, :], 0.0
+                    low_half[:16], acc_ref[0, STEP + tiles * TILE : 2 * STEP + tiles * TILE, :], 0.0
                 )
 
         for ty in range(3):
-            total = acc_s[0:64, 128 * ty : 128 * (ty + 1)]
-            for ii in range(1, 4):
-                total = total + acc_s[
-                    64 * ii : 64 * (ii + 1), 128 * (ii + ty) : 128 * (ii + ty + 1)
-                ]
+            total = (
+                acc_s[64 * (2 - ty) : 64 * (3 - ty), :128]
+                + acc_s[64 * (3 - ty) : 64 * (4 - ty), 128:]
+            )
             taps_ref[ty] = total[:C] + pltpu.roll(total[C:], 96, 1)
 
 
@@ -433,6 +512,14 @@
         ]
     )
 
+    kept = jnp.arange(2 * PLANE, dtype=jnp.int32)[:, None]
+    r, jp, s = (x[None, :] for x in (
+        jnp.arange(ROWS, dtype=jnp.int32) // PLANE,
+        jnp.arange(ROWS, dtype=jnp.int32) % PLANE // STEP,
+        jnp.arange(ROWS, dtype=jnp.int32) % STEP,
+    ))
+    pick = ((kept == jp * STEP + r) | (kept == PLANE + jp * STEP + s)).astype(BF)
+
     def chunk_spec(offset, column, edge):
         def index(t, s):
             n = s[2 * blocks] * tiles + t + offset
@@ -466,6 +553,7 @@
             whole(wb),
             whole(spread),
             whole(place),
+            whole(pick),
             whole(vec),
         ],
         out_specs=[
@@ -476,18 +564,17 @@
             pltpu.VMEM((SPAN, 128), F32),
             pltpu.VMEM((2, SPAN, 128), F32),
             pltpu.VMEM((PLANE, 128), F32),
-            pltpu.VMEM((2, PLANE, 128), F32),
             pltpu.VMEM((2, 3, PLANE, 128), F32),
-            pltpu.VMEM((ROWS, 256), jnp.int32),
+            pltpu.VMEM((PLANE, 128), F32),
+            pltpu.VMEM((2, 3, PLANE, 128), F32),
+            pltpu.VMEM((2, ROWS, 256), F32),
             pltpu.VMEM((ROWS, 256), BF),
             pltpu.VMEM((2, SLABS, ROWS, 128), BF),
-            pltpu.VMEM((SPAN, 8, 128), F32),
-            pltpu.VMEM((SPAN, 8, 128), F32),
             pltpu.VMEM((PLANE, 128), F32),
-            pltpu.VMEM((PLANE, 128), F32),
-            pltpu.VMEM((256, 768), F32),
-            pltpu.VMEM((tiles * TILE + 2 * STEP, 128), F32),
-            pltpu.VMEM((tiles * TILE + 2 * STEP, 128), F32),
+            pltpu.VMEM((3, PLANE, 128), F32),
+            pltpu.VMEM((256, 256), F32),
+            pltpu.VMEM((2, tiles * TILE + 2 * STEP, 128), F32),
+            pltpu.VMEM((2, tiles * TILE + 2 * STEP, 128), F32),
         ],
     )
     return pl.pallas_call(
@@ -513,6 +600,7 @@
         wb,
         spread,
         place,
+        pick,
         vec,
     )
 
@@ -549,12 +637,15 @@
     taps = convolution_weight.reshape(3, 3, C, C).transpose(0, 1, 3, 2)
     wf = jnp.stack(
         [
-            jnp.pad(taps, ((ii, 3 - ii), (jj, 1 - jj), (0, 0), (0, 0)))
-            for ii in range(4)
+            jnp.pad(
+                taps[max(0, 2 - rho) : 4 - rho],
+                ((max(0, rho - 2), max(0, 1 - rho)), (jj, 1 - jj), (0, 0), (0, 0)),
+            )
+            for rho in range(4)
             for jj in range(2)
         ],
         axis=3,
-    ).reshape(768, 256)
+    ).reshape(256, 256)
     wb = wf.T
     vec = jnp.stack([jnp.tile(convolution_bias, 8), jnp.tile(readout, 8)])
     grads, tap_sums = run_tiles(scalars, code_chunks, targets, wf, wb, vec, blocks, tiles)

time: 109 us -> 105 us (0.963)
  Pallas kernels: 46.3 us -> 41.6 us
    pallas_call x1, Pallas kernels: 46.3 us -> 41.6 us  [run_tiles(): pl.pallas_call(functools.partial(tile_kernel, blocks, tiles), grid_spec=g...]
  transfers between devices with their start and end apart: 1 -> 1, of which waited for: 1 -> 1; matrix products, arithmetic and copies ran while one was open for 3% -> 2% of each run, Pallas kernels for 0% -> 0%
where the time goes in v3:
time: 105 us; the launch traced here: 104 us
  Pallas kernels  41.6 us (40%)
  blocking collectives  26.4 us (25%)
  waiting for transfers between devices  17.1 us (16%)
  starting transfers between devices  11.1 us (11%)
  local copies, waits for them, and re-layouts  3.97 us (4%)
  other arithmetic  2.05 us (2%)
    pallas_call x1, Pallas kernels, run_tiles(): pl.pallas_call(functools.partial(tile_kernel, blocks, tiles), grid_spec=g...  41.6 us
    all_to_all x1, blocking collectives, per_device(): received = lax.all_to_all(terms, axes, 0, 0, tiled=True)  26.4 us
    all_to_all x1, waiting for transfers between devices, per_device(): lax.all_to_all(jnp.broadcast_to(packed[None], (2 * blocks, 32, 128)), axe...  17.1 us
    all_to_all x1, starting transfers between devices, per_device(): lax.all_to_all(jnp.broadcast_to(packed[None], (2 * blocks, 32, 128)), axe...  11.1 us
  transfers between devices with their start and end apart: 1, of which 1 were waited for; matrix products, arithmetic and copies ran while one was open for 2% of the time, Pallas kernels for 0%

profile of v3, /device:TPU:0, one launch (start us, length us, event | category | flops | bytes accessed | tf_op | source)
XLA Modules:
  0.0 104.0 jit_solution(3762832643534540911)
XLA Ops:
  0.6 0.0 copy-start
  0.6 0.7 copy-done
  1.4 0.9 convolution_convert_fusion
  2.3 0.1 pad_maximum_fusion.4
  2.4 1.1 %broadcast_in_dim.16 = bf16[128,32,128]{2,1,0:T(8,128)(2,1)} broadcast(bf16[32,128]{1,0:T(8,128)(2,1)S(1)} %pad_maximum_fusion.4), dimensions={1,2} | broadcast | bytes 1056768 | tf_op jit(solution)/shard_map/broadcast_in_dim | solution.py:624
  3.5 0.0 copy-start.2
  3.5 0.0 copy-start.6
  3.5 0.0 copy-start.3
  3.5 0.0 copy-start.4
  3.5 11.1 %all-to-all-start = ((bf16[128,32,128]{2,1,0:T(8,128)(2,1)}), bf16[128,32,128]{2,1,0:T(8,128)(2,1)S(1)}, u32[]{:S(2)}, u32[]{:S(2)}) async-start(bf16[128,32,128]{2,1,0:T(8,128)(2,1)} %broadcast_in_dim.16), calls=%async_computation | async-start | bytes 2097152 | tf_op jit(solution)/shard_map/all_to_all | solution.py:623
  14.7 0.0 copy-done.2
  14.8 0.1 copy.20
  14.8 0.0 copy-start.5
  14.9 0.0 copy-done.6
  14.9 0.1 select_reduce_fusion
  15.0 0.0 copy-done.3
  15.0 0.1 stack_tile.6
  15.1 0.0 copy-done.4
  15.1 0.1 stack_tile.7
  15.3 0.1 bitcast_dynamic-update-slice_fusion.5
  15.3 0.1 bitcast_dynamic-update-slice_fusion.4
  15.5 0.1 bitcast_dynamic-update-slice_fusion.2
  15.6 0.1 bitcast_dynamic-update-slice_fusion
  15.6 0.4 reshape.305
  16.0 0.1 copy.16.wf_ref
  16.2 0.0 copy-done.5
  16.2 0.1 pad_add_fusion.s_ref
  16.3 0.1 compare_convert_fusion
  16.4 0.1 fusion.11
  16.5 0.0 copy-start.1
  16.5 0.1 maximum_bitcast_fusion
  16.5 0.1 pad_maximum_fusion.1.place_ref
  16.6 0.1 fusion.1.pick_ref
  16.7 17.1 %all-to-all-done.row_prev.row_here.row_next.col_prev.col_here.col_next = bf16[128,32,128]{2,1,0:T(8,128)(2,1)S(1)} async-done(((bf16[128,32,128]{2,1,0:T(8,128)(2,1)}), bf16[128,32,128]{2,1,0:T(8,128)(2,1)S(1)}, u32[]{:S(2)}, u32[]{:S(2)}) %all-to-all-start) | async-done | bytes 1048608 | tf_op jit(solution)/shard_map/all_to_all | solution.py:623
  33.8 0.0 copy-done.1
  33.9 41.6 %shard_map.95 = (f32[128,32,128]{2,1,0:T(8,128)S(1)}, f32[3,32,128]{2,1,0:T(8,128)S(1)}) custom-call(s32[130]{0:T(256)S(1)} %pad_add_fusion.s_ref, bf16[128,32,128]{2,1,0:T(8,128)(2,1)S(1)} %all-to-all-done.row_prev.row_here.row_next.col_prev.col_here.col_next, bf16[128,32,128]{2,1,0:T(8,128)(2,1)S(1)} %all-to-all-done.row_prev.row_here.row_next.col_prev.col_here.col_next, ...), custom_call_target="tpu_custom_call" | custom-call | tf_op jit(solution)/shard_map/pallas_call | solution.py:580
  75.4 0.2 convert_element_type.67
  75.7 0.1 div.106
  75.8 0.1 div.108
  76.0 0.2 pad_maximum_fusion
  76.2 26.4 %all_to_all.10 = bf16[128,40,128]{2,1,0:T(8,128)(2,1)S(1)} all-to-all(bf16[128,40,128]{2,1,0:T(8,128)(2,1)S(1)} %pad_maximum_fusion), channel_id=1, replica_groups=mesh['row'=8,'diag'=16] {'row','diag'}, dimensions={0} | all-to-all | bytes 2621440 | tf_op jit(solution)/shard_map/all_to_all | solution.py:659
  102.6 0.2 convert_reduce_fusion
  102.8 0.5 slice_bitcast_fusion
  103.3 0.1 fusion.36
  103.4 0.6 pad_maximum_fusion.3
  (22 shorter events, 0.5 us)
Async XLA Ops:
  0.6 0.8 copy-start
  3.5 11.2 %copy-start.2 = (bf16[9,32,32]{2,1,0:T(8,128)(2,1)S(1)}, bf16[9,32,32]{2,1,0:T(8,128)(2,1)}, u32[]{:S(2)}) copy-start(bf16[9,32,32]{2,1,0:T(8,128)(2,1)} %param.10) | copy-start | bytes 55300
  3.5 11.4 %copy-start.6 = (s32[64]{0:T(128)S(1)}, s32[64]{0:T(128)}, u32[]{:S(2)}) copy-start(s32[64]{0:T(128)} %param.14) | copy-start | bytes 772
  3.5 11.5 %copy-start.3 = (f32[32]{0:T(128)S(1)}, f32[32]{0:T(128)}, u32[]{:S(2)}) copy-start(f32[32]{0:T(128)} %param.11) | copy-start | bytes 388
  3.5 11.6 %copy-start.4 = (f32[32]{0:T(128)S(1)}, f32[32]{0:T(128)}, u32[]{:S(2)}) copy-start(f32[32]{0:T(128)} %param.12) | copy-start | bytes 388
  3.5 30.3 %all-to-all-start = ((bf16[128,32,128]{2,1,0:T(8,128)(2,1)}), bf16[128,32,128]{2,1,0:T(8,128)(2,1)S(1)}, u32[]{:S(2)}, u32[]{:S(2)}) async-start(bf16[128,32,128]{2,1,0:T(8,128)(2,1)} %broadcast_in_dim.16), calls=%async_computation | async-start | bytes 2097152 | tf_op jit(solution)/shard_map/all_to_all | solution.py:623
  14.8 1.4 %copy-start.5 = (s32[64]{0:T(128)S(1)}, s32[64]{0:T(128)}, u32[]{:S(2)}) copy-start(s32[64]{0:T(128)} %param.15) | copy-start | bytes 772
  16.5 17.4 %copy-start.1 = (bf16[8,128,128]{2,1,0:T(8,128)(2,1)S(1)}, bf16[8,128,128]{2,1,0:T(8,128)(2,1)}, u32[]{:S(2)}) copy-start(bf16[8,128,128]{2,1,0:T(8,128)(2,1)} %tgt_ref.1) | copy-start | bytes 786436

commit v4 on v3

--- a/solution.py
+++ b/solution.py
@@ -65,12 +65,8 @@
     blocks,
     tiles,
     s_ref,
-    row_prev,
-    row_here,
-    row_next,
-    col_prev,
-    col_here,
-    col_next,
+    mine_ref,
+    theirs_ref,
     tgt_ref,
     wf_ref,
     wb_ref,
@@ -78,7 +74,8 @@
     place_ref,
     pick_ref,
     vec_ref,
-    grads_ref,
+    keep_ref,
+    send_ref,
     taps_ref,
     u_row,
     w_row,
@@ -94,6 +91,7 @@
     acc_s,
     row_acc,
     col_acc,
+    grads_s,
 ):
     g = pl.program_id(0)
     new = g % 2
@@ -117,16 +115,24 @@
             dist = TILE * d - 64 * ig + 32 * jp + s - r + 16 * (jj - ii)
             dist_s[ig] = jnp.where(dist >= 0, dist, 1 << 20).astype(F32)
 
-    def codes(prev, here, after):
+    core = s_ref[2 * blocks + 1] % 2
+
+    def codes(n):
         left, right = spread_ref[0], spread_ref[1]
+
+        def chunk(block, h, rows):
+            slot = s_ref[jnp.clip(block, 0, blocks - 1)]
+            return jnp.where(core == h, mine_ref[slot, rows, :], theirs_ref[slot, rows, :])
+
+        first_half, second_half = (chunk(n, h, slice(0, 32)) for h in range(2))
         return jnp.concatenate(
             [
-                dot(prev[0], right),
-                dot(here[0], left),
-                dot(here[0], right),
-                dot(here[1], left),
-                dot(here[1], right),
-                dot(after[0], left),
+                dot(chunk(n - 1, 1, slice(16, 32)), right),
+                dot(first_half, left),
+                dot(first_half, right),
+                dot(second_half, left),
+                dot(second_half, right),
+                dot(chunk(n + 1, 0, slice(0, 16)), left),
             ],
             axis=0,
         )
@@ -135,10 +141,10 @@
         return 0 if i == 0 else (2 if i == SLABS - 1 else 1)
 
     def prepare():
-        row_codes = codes(row_prev, row_here, row_next)
+        row_codes = codes(first + g)
         u_row[...] = row_codes[:, :128]
         w_row[new] = row_codes[:, 128:]
-        col_codes = codes(col_prev, col_here, col_next).reshape(SLABS, STEP, 256)
+        col_codes = codes(first + g + d).reshape(SLABS, STEP, 256)
         group = lax.broadcasted_iota(jnp.int32, (STEP, 256), 1) // C % 4
         for jp in range(PAIRS):
             window = col_codes[2 * jp]
@@ -209,7 +215,7 @@
         c0_s[...] = jnp.zeros_like(c0_s)
         c1_s[...] = jnp.zeros_like(c1_s)
 
-        turned = tgt_ref[0].astype(F32).T.reshape(PAIRS, 2, STEP, TILE)
+        turned = tgt_ref[t].astype(F32).T.reshape(PAIRS, 2, STEP, TILE)
         sides = [turned[:, jj].reshape(PLANE, TILE) for jj in range(2)]
 
         def make_target(r):
@@ -443,7 +449,7 @@
 
     @pl.when(g == tiles)
     def _():
-        grads_ref[...] = jnp.zeros_like(grads_ref)
+        grads_s[...] = jnp.zeros_like(grads_s)
         low_half = lax.broadcasted_iota(jnp.int32, (32, 128), 1) < 64
         even = lax.broadcasted_iota(jnp.int32, row_acc.shape[1:], 1) // C % 2 == 0
         for acc_ref in (row_acc, col_acc):
@@ -459,7 +465,7 @@
                 for h in range(2):
                     top = acc_ref[0, pl.ds(begin + 64 * h, 32), :]
                     bottom = acc_ref[0, pl.ds(begin + 64 * h + 32, 32), :]
-                    grads_ref[2 * slot + h] += jnp.where(low_half, top, bottom)
+                    grads_s[(h + core) % 2, slot] += jnp.where(low_half, top, bottom)
 
         for acc_ref, base in ((row_acc, first), (col_acc, first + d)):
             for k in range(tiles):
@@ -468,17 +474,19 @@
             @pl.when((base > 0) & (base <= blocks))
             def _():
                 slot = s_ref[jnp.clip(base - 1, 0, blocks - 1)]
-                grads_ref[2 * slot + 1, pl.ds(16, 16), :] += jnp.where(
+                grads_s[(1 + core) % 2, slot, pl.ds(16, 16), :] += jnp.where(
                     low_half[:16], 0.0, acc_ref[0, 0:STEP, :]
                 )
 
             @pl.when(base + tiles < blocks)
             def _():
                 slot = s_ref[jnp.minimum(base + tiles, blocks - 1)]
-                grads_ref[2 * slot, pl.ds(0, 16), :] += jnp.where(
+                grads_s[core, slot, pl.ds(0, 16), :] += jnp.where(
                     low_half[:16], acc_ref[0, STEP + tiles * TILE : 2 * STEP + tiles * TILE, :], 0.0
                 )
 
+        keep_ref[...] = grads_s[0]
+        send_ref[...] = grads_s[1].astype(BF)
         for ty in range(3):
             total = (
                 acc_s[64 * (2 - ty) : 64 * (3 - ty), :128]
@@ -487,7 +495,7 @@
             taps_ref[ty] = total[:C] + pltpu.roll(total[C:], 96, 1)
 
 
-def run_tiles(scalars, code_chunks, targets, wf, wb, vec, blocks, tiles):
+def run_tiles(scalars, mine, theirs, targets, wf, wb, vec, blocks, tiles):
     lane = jnp.arange(256, dtype=jnp.int32)
     source = lane // 128 * C + lane % C
     depth = jnp.arange(128, dtype=jnp.int32)
@@ -520,20 +528,6 @@
     ))
     pick = ((kept == jp * STEP + r) | (kept == PLANE + jp * STEP + s)).astype(BF)
 
-    def chunk_spec(offset, column, edge):
-        def index(t, s):
-            n = s[2 * blocks] * tiles + t + offset
-            if column:
-                n = n + s[2 * blocks + 1]
-            n = s[jnp.clip(n, 0, blocks - 1)]
-            if edge < 0:
-                return (2 * n + 1, 1, 0)
-            if edge > 0:
-                return (2 * n, 0, 0)
-            return (n, 0, 0)
-
-        return pl.BlockSpec((1, STEP, 128) if edge else (2, 32, 128), index)
-
     def whole(x):
         zeros = (0,) * x.ndim
         return pl.BlockSpec(x.shape, lambda t, s: zeros)
@@ -542,13 +536,9 @@
         num_scalar_prefetch=1,
         grid=(tiles + 1,),
         in_specs=[
-            chunk_spec(-1, False, -1),
-            chunk_spec(0, False, 0),
-            chunk_spec(1, False, 1),
-            chunk_spec(-1, True, -1),
-            chunk_spec(0, True, 0),
-            chunk_spec(1, True, 1),
-            pl.BlockSpec((1, TILE, TILE), lambda t, s: (jnp.maximum(t - 1, 0), 0, 0)),
+            whole(mine),
+            whole(theirs),
+            whole(targets),
             whole(wf),
             whole(wb),
             whole(spread),
@@ -557,7 +547,8 @@
             whole(vec),
         ],
         out_specs=[
-            pl.BlockSpec((2 * blocks, 32, 128), lambda t, s: (0, 0, 0)),
+            pl.BlockSpec((blocks, 32, 128), lambda t, s: (0, 0, 0)),
+            pl.BlockSpec((blocks, 32, 128), lambda t, s: (0, 0, 0)),
             pl.BlockSpec((3, C, 128), lambda t, s: (0, 0, 0)),
         ],
         scratch_shapes=[
@@ -575,13 +566,15 @@
             pltpu.VMEM((256, 256), F32),
             pltpu.VMEM((2, tiles * TILE + 2 * STEP, 128), F32),
             pltpu.VMEM((2, tiles * TILE + 2 * STEP, 128), F32),
+            pltpu.VMEM((2, blocks, 32, 128), F32),
         ],
     )
     return pl.pallas_call(
         functools.partial(tile_kernel, blocks, tiles),
         grid_spec=grid_spec,
         out_shape=[
-            jax.ShapeDtypeStruct((2 * blocks, 32, 128), F32),
+            jax.ShapeDtypeStruct((blocks, 32, 128), F32),
+            jax.ShapeDtypeStruct((blocks, 32, 128), BF),
             jax.ShapeDtypeStruct((3, C, 128), F32),
         ],
         compiler_params=pltpu.CompilerParams(
@@ -589,12 +582,8 @@
         ),
     )(
         scalars,
-        code_chunks,
-        code_chunks,
-        code_chunks,
-        code_chunks,
-        code_chunks,
-        code_chunks,
+        mine,
+        theirs,
         targets,
         wf,
         wb,
@@ -620,9 +609,19 @@
     axes = ("row", "diag")
     code_local = dot(bins_x, proj_weight).astype(BF)
     packed = jnp.concatenate([code_local[:32], code_local[32:]], axis=1)
-    code_chunks = lax.all_to_all(
-        jnp.broadcast_to(packed[None], (2 * blocks, 32, 128)), axes, 0, 0, tiled=True
-    )
+    core = lax.axis_index("diag") % 2
+    peers = lax.axis_size("row") * lax.axis_size("diag")
+    same_core = [list(range(c, peers, 2)) for c in range(2)]
+    swap = [(i, i ^ 1) for i in range(lax.axis_size("diag"))]
+    mine = lax.all_to_all(
+        jnp.broadcast_to(packed[None], (blocks, 32, 128)),
+        axes,
+        0,
+        0,
+        axis_index_groups=same_core,
+        tiled=True,
+    )
+    theirs = lax.ppermute(mine, "diag", swap)
     positions = jnp.arange(blocks, dtype=jnp.int32)
     inverse = jnp.sum(
         jnp.where(block_order[:, None] == positions[None, :], positions[:, None], 0), axis=0
@@ -648,18 +647,25 @@
     ).reshape(256, 256)
     wb = wf.T
     vec = jnp.stack([jnp.tile(convolution_bias, 8), jnp.tile(readout, 8)])
-    grads, tap_sums = run_tiles(scalars, code_chunks, targets, wf, wb, vec, blocks, tiles)
+    keep, send, tap_sums = run_tiles(scalars, mine, theirs, targets, wf, wb, vec, blocks, tiles)
     tap_flat = (
         tap_sums[:, :, : 3 * C].reshape(3, C, 3, C).transpose(0, 2, 1, 3).reshape(2 * blocks, -1)
         / blocks
     )
     owned = tap_flat.shape[1]
-    tap_rows = jnp.pad(tap_flat, ((0, 0), (0, 1024 - owned))).reshape(2 * blocks, 8, 128)
-    terms = jnp.concatenate([grads.astype(BF), tap_rows.astype(BF)], axis=1)
-    received = lax.all_to_all(terms, axes, 0, 0, tiled=True)
-    mine = jnp.sum(received.astype(F32), axis=0)
-    codes_grad = jnp.concatenate([mine[:32, :64], mine[:32, 64:]], axis=0)
-    conv_grad = mine[32, :owned]
+    tap_rows = jnp.pad(tap_flat, ((0, 0), (0, 1024 - owned))).reshape(blocks, 2, 8, 128)
+    tap_first, tap_second = tap_rows[:, 0], tap_rows[:, 1]
+    tap_keep = jnp.where(core == 0, tap_first, tap_second)
+    tap_send = jnp.where(core == 0, tap_second, tap_first)
+    sent = jnp.concatenate([send, tap_send.astype(BF)], axis=1)
+    other = lax.ppermute(sent, "diag", swap)
+    terms = jnp.concatenate([keep, tap_keep], axis=1) + other.astype(F32)
+    received = lax.all_to_all(
+        terms.astype(BF), axes, 0, 0, axis_index_groups=same_core, tiled=True
+    )
+    total = jnp.sum(received.astype(F32), axis=0)
+    codes_grad = jnp.concatenate([total[:32, :64], total[:32, 64:]], axis=0)
+    conv_grad = total[32, :owned]
     return (codes_grad, conv_grad)
 
 

time: 105 us -> 95.8 us (0.912)
  blocking collectives: 26.4 us -> 19.4 us
  waiting for transfers between devices: 17.1 us -> 14.6 us
    all_to_all x1, blocking collectives: 26.4 us -> 19.4 us  [per_device(): lax.all_to_all(terms.astype(BF), axes, 0, 0, axis_index_groups=same_core,...]
    all_to_all x1, waiting for transfers between devices: 17.1 us -> 11.6 us  [per_device(): lax.all_to_all(jnp.broadcast_to(packed[None], (blocks, 32, 128)), axes, 0...]
    ppermute x0 -> x2, waiting for transfers between devices: none -> 3 us  [the longest x1 1.9 us: per_device(): other = lax.ppermute(sent, 'diag', swap)]
  transfers between devices with their start and end apart: 1 -> 3, of which waited for: 1 -> 3; matrix products, arithmetic and copies ran while one was open for 2% -> 2% of each run, Pallas kernels for 0% -> 0%
where the time goes in v4:
time: 95.8 us; the launch traced here: 95.5 us
  Pallas kernels  42.3 us (44%)
  blocking collectives  19.4 us (20%)
  waiting for transfers between devices  14.6 us (15%)
  starting transfers between devices  11.7 us (12%)
  local copies, waits for them, and re-layouts  3.77 us (4%)
  other arithmetic  1.82 us (2%)
    pallas_call x1, Pallas kernels, run_tiles(): pl.pallas_call(functools.partial(tile_kernel, blocks, tiles), grid_spec=g...  42.3 us
    all_to_all x1, blocking collectives, per_device(): lax.all_to_all(terms.astype(BF), axes, 0, 0, axis_index_groups=same_core,...  19.4 us
    all_to_all x1, waiting for transfers between devices, per_device(): lax.all_to_all(jnp.broadcast_to(packed[None], (blocks, 32, 128)), axes, 0...  11.6 us
    all_to_all x1, starting transfers between devices, per_device(): lax.all_to_all(jnp.broadcast_to(packed[None], (blocks, 32, 128)), axes, 0...  11.5 us
  transfers between devices with their start and end apart: 3, of which 3 were waited for; matrix products, arithmetic and copies ran while one was open for 2% of the time, Pallas kernels for 0%

profile of v4, /device:TPU:0, one launch (start us, length us, event | category | flops | bytes accessed | tf_op | source)
XLA Modules:
  0.0 95.5 jit_solution(14728067352866005206)
XLA Ops:
  0.6 0.0 copy-start
  0.6 0.0 copy-start.2
  0.7 0.7 copy-done
  1.4 0.9 convolution_convert_fusion
  2.3 0.1 pad_maximum_fusion.4
  2.4 0.0 copy-start.6
  2.4 0.0 copy-start.3
  2.4 0.0 copy-start.4
  2.4 0.9 broadcast_in_dim.16
  3.2 11.5 %all-to-all-start = ((bf16[64,32,128]{2,1,0:T(8,128)(2,1)}), bf16[64,32,128]{2,1,0:T(8,128)(2,1)S(1)}, u32[]{:S(2)}, u32[]{:S(2)}) async-start(bf16[64,32,128]{2,1,0:T(8,128)(2,1)} %broadcast_in_dim.16), calls=%async_computation | async-start | bytes 1048576 | tf_op jit(solution)/shard_map/all_to_all | solution.py:616
  14.8 0.0 copy-done.2
  14.8 0.1 copy.26
  14.9 0.0 copy-start.5
  15.0 0.0 copy-done.6
  15.0 0.1 select_reduce_fusion
  15.1 0.0 copy-done.3
  15.1 0.1 stack_tile.6
  15.2 0.0 copy-done.4
  15.2 0.1 stack_tile.7
  15.4 0.1 bitcast_dynamic-update-slice_fusion.5
  15.4 0.1 bitcast_dynamic-update-slice_fusion.4
  15.5 0.1 bitcast_dynamic-update-slice_fusion.2
  15.6 0.1 bitcast_dynamic-update-slice_fusion
  15.8 0.1 compare_convert_fusion
  15.9 0.1 fusion.13
  16.0 11.6 %all-to-all-done.mine_ref = bf16[64,32,128]{2,1,0:T(8,128)(2,1)S(1)} async-done(((bf16[64,32,128]{2,1,0:T(8,128)(2,1)}), bf16[64,32,128]{2,1,0:T(8,128)(2,1)S(1)}, u32[]{:S(2)}, u32[]{:S(2)}) %all-to-all-start) | async-done | bytes 524320 | tf_op jit(solution)/shard_map/all_to_all | solution.py:616
  27.6 0.0 collective-permute-start
  27.6 0.0 copy-done.5
  27.6 0.1 pad_add_fusion.s_ref
  27.7 0.4 reshape.309
  28.0 0.1 copy.18.wf_ref
  28.2 0.1 maximum_bitcast_fusion
  28.2 0.0 copy-start.1
  28.2 0.1 pad_maximum_fusion.place_ref
  28.3 0.1 fusion.2.pick_ref
  28.4 1.1 %collective-permute-done.theirs_ref = bf16[64,32,128]{2,1,0:T(8,128)(2,1)S(1)} collective-permute-done((bf16[64,32,128]{2,1,0:T(8,128)(2,1)S(1)}, bf16[64,32,128]{2,1,0:T(8,128)(2,1)S(1)}, u32[]{:S(2)}, u32[]{:S(2)}) %collective-permute-start) | collective-permute-done | bytes 524320 | tf_op jit(solution)/shard_map/ppermute | solution.py:624
  29.5 0.0 copy-done.1
  29.5 42.3 %shard_map.95 = (f32[64,32,128]{2,1,0:T(8,128)S(1)}, bf16[64,32,128]{2,1,0:T(8,128)(2,1)S(1)}, f32[3,32,128]{2,1,0:T(8,128)S(1)}) custom-call(s32[130]{0:T(256)S(1)} %pad_add_fusion.s_ref, bf16[64,32,128]{2,1,0:T(8,128)(2,1)S(1)} %all-to-all-done.mine_ref, bf16[64,32,128]{2,1,0:T(8,128)(2,1)S(1)} %collective-permute-done.theirs_ref, ...), custom_call_target="tpu_custom_call" | custom-call | tf_op jit(solution)/shard_map/pallas_call | solution.py:572
  71.8 0.1 div.106
  72.0 0.1 div.108
  72.1 0.1 pad_bitcast_fusion
  72.2 0.1 copy.24
  72.3 0.1 pad_maximum_fusion.1
  72.4 0.2 collective-permute-start.1
  72.6 1.9 %collective-permute-done.1 = bf16[64,40,128]{2,1,0:T(8,128)(2,1)S(1)} collective-permute-done((bf16[64,40,128]{2,1,0:T(8,128)(2,1)S(1)}, bf16[64,40,128]{2,1,0:T(8,128)(2,1)S(1)}, u32[]{:S(2)}, u32[]{:S(2)}) %collective-permute-start.1) | collective-permute-done | bytes 655392 | tf_op jit(solution)/shard_map/ppermute | solution.py:661
  74.5 0.2 fusion
  74.7 19.4 %all_to_all.10 = bf16[64,40,128]{2,1,0:T(8,128)(2,1)S(1)} all-to-all(bf16[64,40,128]{2,1,0:T(8,128)(2,1)S(1)} %fusion), channel_id=1, replica_groups={{0,2,4,6,8,10,12,14,16,18,20,22,24,26,28,30,32,34,36,38,40,42,44,46,48,..., dimensions={0} | all-to-all | bytes 1310720 | tf_op jit(solution)/shard_map/all_to_all | solution.py:663
  94.2 0.1 convert_reduce_fusion
  94.3 0.5 slice_bitcast_fusion.2
  94.8 0.1 fusion.38
  94.9 0.6 pad_maximum_fusion.3
  (22 shorter events, 0.4 us)
Async XLA Ops:
  0.6 0.8 copy-start
  0.6 14.2 %copy-start.2 = (bf16[9,32,32]{2,1,0:T(8,128)(2,1)S(1)}, bf16[9,32,32]{2,1,0:T(8,128)(2,1)}, u32[]{:S(2)}) copy-start(bf16[9,32,32]{2,1,0:T(8,128)(2,1)} %param.10) | copy-start | bytes 55300
  2.4 12.6 %copy-start.6 = (s32[64]{0:T(128)S(1)}, s32[64]{0:T(128)}, u32[]{:S(2)}) copy-start(s32[64]{0:T(128)} %param.14) | copy-start | bytes 772
  2.4 12.7 %copy-start.3 = (f32[32]{0:T(128)S(1)}, f32[32]{0:T(128)}, u32[]{:S(2)}) copy-start(f32[32]{0:T(128)} %param.11) | copy-start | bytes 388
  2.4 12.8 %copy-start.4 = (f32[32]{0:T(128)S(1)}, f32[32]{0:T(128)}, u32[]{:S(2)}) copy-start(f32[32]{0:T(128)} %param.12) | copy-start | bytes 388
  3.2 24.4 %all-to-all-start = ((bf16[64,32,128]{2,1,0:T(8,128)(2,1)}), bf16[64,32,128]{2,1,0:T(8,128)(2,1)S(1)}, u32[]{:S(2)}, u32[]{:S(2)}) async-start(bf16[64,32,128]{2,1,0:T(8,128)(2,1)} %broadcast_in_dim.16), calls=%async_computation | async-start | bytes 1048576 | tf_op jit(solution)/shard_map/all_to_all | solution.py:616
  14.9 12.7 %copy-start.5 = (s32[64]{0:T(128)S(1)}, s32[64]{0:T(128)}, u32[]{:S(2)}) copy-start(s32[64]{0:T(128)} %param.15) | copy-start | bytes 772
  27.6 1.9 %collective-permute-start = (bf16[64,32,128]{2,1,0:T(8,128)(2,1)S(1)}, bf16[64,32,128]{2,1,0:T(8,128)(2,1)S(1)}, u32[]{:S(2)}, u32[]{:S(2)}) collective-permute-start(bf16[64,32,128]{2,1,0:T(8,128)(2,1)S(1)} %all-to-all-done.mine_ref), channel_id=1, source_target_pairs={{0,1},{1,0},{2,3},{3,2},{4,5},{5,4},{6,7},{7,6},{8,9},{9,8},{10,11... | collective-permute-start | bytes 1572872 | tf_op jit(solution)/shard_map/ppermute | solution.py:624
  28.2 1.3 %copy-start.1 = (bf16[8,128,128]{2,1,0:T(8,128)(2,1)S(1)}, bf16[8,128,128]{2,1,0:T(8,128)(2,1)}, u32[]{:S(2)}) copy-start(bf16[8,128,128]{2,1,0:T(8,128)(2,1)} %tgt_ref.1) | copy-start | bytes 786436
  72.4 2.2 %collective-permute-start.1 = (bf16[64,40,128]{2,1,0:T(8,128)(2,1)S(1)}, bf16[64,40,128]{2,1,0:T(8,128)(2,1)S(1)}, u32[]{:S(2)}, u32[]{:S(2)}) collective-permute-start(bf16[64,40,128]{2,1,0:T(8,128)(2,1)S(1)} %pad_maximum_fusion.1), channel_id=1, source_target_pairs={{0,1},{1,0},{2,3},{3,2},{4,5},{5,4},{6,7},{7,6},{8,9},{9,8},{10,11... | collective-permute-start | bytes 1966088 | tf_op jit(solution)/shard_map/ppermute | solution.py:661

commit v5 on v4

--- a/solution.py
+++ b/solution.py
@@ -19,6 +19,7 @@
 CHUNK = 512
 MPIECE = 512
 GROUP = 8
+TOGETHER = 1
 
 SQRT_HALF = 0.7071067811865476
 HALF_LOG2E = -0.7213475204444817
@@ -140,37 +141,39 @@
     def kind(i):
         return 0 if i == 0 else (2 if i == SLABS - 1 else 1)
 
-    def prepare():
-        row_codes = codes(first + g)
-        u_row[...] = row_codes[:, :128]
-        w_row[new] = row_codes[:, 128:]
-        col_codes = codes(first + g + d).reshape(SLABS, STEP, 256)
+    def prepare(q):
+        here = first + g * TOGETHER + q
+        slot = new * TOGETHER + q
+        row_codes = codes(here)
+        u_row[q] = row_codes[:, :128]
+        w_row[slot] = row_codes[:, 128:]
+        col_codes = codes(here + d).reshape(SLABS, STEP, 256)
         group = lax.broadcasted_iota(jnp.int32, (STEP, 256), 1) // C % 4
         for jp in range(PAIRS):
             window = col_codes[2 * jp]
             for m in range(1, 4):
                 window = jnp.where(group == m, col_codes[2 * jp + m], window)
-            uq_s[jp * STEP : (jp + 1) * STEP, :] = window[:, :128]
-            wq_s[new, 1, jp * STEP : (jp + 1) * STEP, :] = window[:, 128:]
+            uq_s[q, jp * STEP : (jp + 1) * STEP, :] = window[:, :128]
+            wq_s[slot, 1, jp * STEP : (jp + 1) * STEP, :] = window[:, 128:]
         line = lax.broadcasted_iota(jnp.int32, (PLANE, 128), 0)
         lane = lax.broadcasted_iota(jnp.int32, (PLANE, 128), 1)
         at_left = (line < STEP) & (lane < C)
         at_right = (line >= PLANE - STEP) & (lane >= 3 * C)
         for k in range(3):
-            ar = first + g - 1 + k
+            ar = here - 1 + k
 
             def inside(cb):
                 ok = (ar >= 0) & (ar < blocks) & (cb >= ar) & (cb - ar < BAND) & (cb < blocks)
                 return jnp.where(ok, 1.0, 0.0).astype(F32)
 
-            bg = first + g + d
-            mask_s[new, k] = jnp.where(
+            bg = here + d
+            mask_s[slot, k] = jnp.where(
                 at_left, inside(bg - 1), jnp.where(at_right, inside(bg + 1), inside(bg))
             )
-        plain_w = wq_s[new, 1]
-        wq_plain[...] = plain_w
+        plain_w = wq_s[slot, 1]
+        wq_plain[q] = plain_w
         for k in range(3):
-            wq_s[new, k] = plain_w * mask_s[new, k]
+            wq_s[slot, k] = plain_w * mask_s[slot, k]
 
     def edged(value, which, k):
         mask = mask_s.at[which, k]
@@ -185,20 +188,23 @@
             axis=0,
         )
 
-    def make_map(i, r):
-        u = u_row[pl.ds(i * STEP + r, 1), :]
-        w = w_row[new, pl.ds(i * STEP + r, 1), :]
-        value = edged((u + uq_s[...]) + w * wq_plain[...], new, kind(i))
-        x_s[new, i, pl.ds(r * PLANE, PLANE), :] = value.astype(BF)
+    def make_map(q, i, r):
+        slot = new * TOGETHER + q
+        u = u_row[q, pl.ds(i * STEP + r, 1), :]
+        w = w_row[slot, pl.ds(i * STEP + r, 1), :]
+        value = edged((u + uq_s[q]) + w * wq_plain[q], slot, kind(i))
+        x_s[slot, i, pl.ds(r * PLANE, PLANE), :] = value.astype(BF)
 
     def make_maps(r, carry):
-        for i in range(SLABS):
-            make_map(i, r)
+        for q in range(TOGETHER):
+            for i in range(SLABS):
+                make_map(q, i, r)
         return carry
 
     @pl.when(g == 0)
     def _():
-        prepare()
+        for q in range(TOGETHER):
+            prepare(q)
         lax.fori_loop(0, STEP, make_maps, 0)
 
     bias = vec_ref[0:1, :]
@@ -207,13 +213,14 @@
     read_density = read * INV_SQRT_TAU
     planes = CHUNK // PLANE
 
-    def tile(t):
-        prepare()
+    def tile(q):
+        t = (g - 1) * TOGETHER + q
+        slot = old * TOGETHER + q
         a = first + t
         b = a + d
         reach = s_ref[blocks + a]
-        c0_s[...] = jnp.zeros_like(c0_s)
-        c1_s[...] = jnp.zeros_like(c1_s)
+        c0_s[q] = jnp.zeros((PLANE, 128), F32)
+        c1_s[q] = jnp.zeros((3, PLANE, 128), F32)
 
         turned = tgt_ref[t].astype(F32).T.reshape(PAIRS, 2, STEP, TILE)
         sides = [turned[:, jj].reshape(PLANE, TILE) for jj in range(2)]
@@ -221,7 +228,7 @@
         def make_target(r):
             for jj in range(2):
                 value = sides[jj] if r == 0 else pltpu.roll(sides[jj], TILE - r, 1)
-                tgt_s[r * PLANE : (r + 1) * PLANE, TILE * jj : TILE * (jj + 1)] = value.astype(BF)
+                tgt_s[q, r * PLANE : (r + 1) * PLANE, TILE * jj : TILE * (jj + 1)] = value.astype(BF)
 
         n = ROWS // CHUNK
         todo = [(ch, ig) for ch in range(n) for ig in range(2)]
@@ -229,7 +236,7 @@
 
         def pair(ch, k):
             rows = pl.ds(ch * CHUNK, CHUNK)
-            return jnp.concatenate([x_s[old, 2 * k + i, rows, :] for i in range(2)], axis=1)
+            return jnp.concatenate([x_s[slot, 2 * k + i, rows, :] for i in range(2)], axis=1)
 
         def forward(m):
             ch, ig = todo[m]
@@ -264,10 +271,8 @@
                 read_cdf = half_read * lax.erf(x) + half_read
                 value = v * read_cdf
                 high = value.astype(BF)
-                low = (value - high.astype(F32)).astype(BF)
                 parts[m, begin] = (
                     high,
-                    low,
                     read_cdf + (read_density * v) * jnp.exp2(v * (v * HALF_LOG2E)),
                 )
 
@@ -283,8 +288,7 @@
                 terms = jnp.concatenate(
                     [
                         jnp.concatenate([x[0] for x in pieces], axis=0),
-                        jnp.concatenate([x[1] for x in pieces], axis=0),
-                        tgt_s[pl.ds(ch * CHUNK + base, MPIECE), :],
+                        tgt_s[q, pl.ds(ch * CHUNK + base, MPIECE), :],
                     ],
                     axis=1,
                 )
@@ -295,7 +299,7 @@
                 keep = dist_s[ig, pl.ds(ch * CHUNK + begin, PLANE), :] <= farthest
                 miss = out[base][begin - base : begin - base + PLANE]
                 err = jnp.where(keep, miss, 0.0) * TILE ** (-0.5)
-                grads[m, begin] = (err * parts[m, begin][2]).astype(BF)
+                grads[m, begin] = (err * parts[m, begin][1]).astype(BF)
 
             todo_list = []
             for base in range(0, CHUNK, MPIECE):
@@ -332,7 +336,7 @@
                     i = 2 * k + half
                     value = out[:, 128 * half : 128 * (half + 1)]
                     rows = value[:PLANE].reshape(PAIRS, STEP, 128)
-                    mask = mask_s.at[old, kind(i)]
+                    mask = mask_s.at[slot, kind(i)]
                     total = rows[0] * mask[0:1, :] + rows[PAIRS - 1] * mask[PLANE - 1 : PLANE, :]
                     for jp in range(1, PAIRS - 1):
                         total = total + rows[jp] * mask[STEP : STEP + 1, :]
@@ -341,8 +345,8 @@
                     if kind(i) == 1:
                         middle = value[PLANE:] if middle is None else middle + value[PLANE:]
                     else:
-                        c0_s[...] += value[PLANE:] * mask[...]
-            c0_s[...] += middle * mask_s[old, 1]
+                        c0_s[q] += value[PLANE:] * mask[...]
+            c0_s[q] += middle * mask_s[slot, 1]
 
         def sides_of(m, which):
             ch, ig = todo[m]
@@ -375,15 +379,15 @@
 
             def piece(k, half, begin):
                 i = 2 * k + half
-                c1 = c1_s[kind(i)]
-                wq = wq_s[old, kind(i)]
+                c1 = c1_s[q, kind(i)]
+                wq = wq_s[slot, kind(i)]
                 r1 = []
                 for rr in range(begin, begin + GROUP):
                     p = i * STEP + ch * planes + rr
                     dx = totals[k][rr * PLANE : (rr + 1) * PLANE, 128 * half : 128 * (half + 1)]
-                    c1 = c1 + dx * w_row[old, p : p + 1, :]
+                    c1 = c1 + dx * w_row[slot, p : p + 1, :]
                     r1.append(jnp.sum((dx * wq).reshape(PLANE // 8, 8, 128), axis=0))
-                c1_s[kind(i)] = c1
+                c1_s[q, kind(i)] = c1
                 rows = pl.ds(pl.multiple_of(t * TILE, TILE) + i * STEP + ch * planes + begin, 8)
                 row_acc[1, rows, :] += rows_of_sums(r1)
 
@@ -399,27 +403,6 @@
                 ]
             return out
 
-        targets = [functools.partial(make_target, r) for r in range(STEP)]
-        fresh = [functools.partial(make_map, i, r) for r in range(STEP) for i in range(SLABS)]
-        units = len(todo)
-        steps = units + 3
-        for m in range(steps):
-            share = fresh[len(fresh) * m // steps : len(fresh) * (m + 1) // steps]
-            tgt_now = targets[STEP * m // 2 : STEP * (m + 1) // 2] if m < 2 else []
-            weave(
-                forward(m) if m < units else [],
-                slope(m - 1) if 0 <= m - 1 < units else [],
-                error(m - 2) if 0 <= m - 2 < units else [],
-                [functools.partial(joined, m - 3), functools.partial(plain, m - 3)]
-                + taps(m - 3)
-                + back(m - 3)
-                if m >= 3
-                else [],
-                share,
-                tgt_now,
-            )
-
-        here = pl.ds(pl.multiple_of(t * TILE, TILE), SPAN)
         group = lax.broadcasted_iota(jnp.int32, (STEP, 128), 1) // C
 
         def unwind(ref):
@@ -436,18 +419,63 @@
                     pieces.append(value)
             return jnp.concatenate(pieces, axis=0)
 
-        plain_back()
-        c1_s[0] = (
-            c1_s[0] * mask_s[old, 0] + c1_s[1] * mask_s[old, 1] + c1_s[2] * mask_s[old, 2]
-        )
-        col_acc[0, here, :] += unwind(c0_s)
-        col_acc[1, here, :] += unwind(c1_s.at[0])
+        def finish():
+            plain_back()
+            here = pl.ds(pl.multiple_of(t * TILE, TILE), SPAN)
+            c1_s[q, 0] = (
+                c1_s[q, 0] * mask_s[slot, 0]
+                + c1_s[q, 1] * mask_s[slot, 1]
+                + c1_s[q, 2] * mask_s[slot, 2]
+            )
+            col_acc[0, here, :] += unwind(c0_s.at[q])
+            col_acc[1, here, :] += unwind(c1_s.at[q, 0])
+
+        targets = [functools.partial(make_target, r) for r in range(STEP)]
+
+        def step(m):
+            out = []
+            if 0 <= m < units:
+                out.append(forward(m))
+            if 0 <= m - 1 < units:
+                out.append(slope(m - 1))
+            if 0 <= m - 2 < units:
+                out.append(error(m - 2))
+            if 0 <= m - 3 < units:
+                out.append(
+                    [functools.partial(joined, m - 3), functools.partial(plain, m - 3)]
+                    + taps(m - 3)
+                    + back(m - 3)
+                    + ([finish] if m - 3 == units - 1 else [])
+                )
+            if m in (0, 1):
+                out.append(targets[STEP * m // 2 : STEP * (m + 1) // 2])
+            return out
+
+        units = len(todo)
+        return step
+
+    def group_of_tiles():
+        for q in range(TOGETHER):
+            prepare(q)
+        fresh = [
+            functools.partial(make_map, q, i, r)
+            for q in range(TOGETHER)
+            for r in range(STEP)
+            for i in range(SLABS)
+        ]
+        tile_steps = [tile(q) for q in range(TOGETHER)]
+        units = 2 * (ROWS // CHUNK)
+        steps = units * TOGETHER + 3
+        for m in range(steps):
+            share = fresh[len(fresh) * m // steps : len(fresh) * (m + 1) // steps]
+            lists = [x for q in range(TOGETHER) for x in tile_steps[q](m - units * q)]
+            weave(*lists, share)
 
     @pl.when(g > 0)
     def _():
-        tile(g - 1)
-
-    @pl.when(g == tiles)
+        group_of_tiles()
+
+    @pl.when(g == tiles // TOGETHER)
     def _():
         grads_s[...] = jnp.zeros_like(grads_s)
         low_half = lax.broadcasted_iota(jnp.int32, (32, 128), 1) < 64
@@ -506,7 +534,7 @@
     place = jnp.stack(
         [
             jnp.concatenate(
-                [ones.astype(BF), ones.astype(BF)]
+                [ones.astype(BF)]
                 + [
                     -(
                         (depth[:, None] == 16 * (4 * ig + lane[None, :] // 64))
@@ -534,7 +562,7 @@
 
     grid_spec = pltpu.PrefetchScalarGridSpec(
         num_scalar_prefetch=1,
-        grid=(tiles + 1,),
+        grid=(tiles // TOGETHER + 1,),
         in_specs=[
             whole(mine),
             whole(theirs),
@@ -552,17 +580,17 @@
             pl.BlockSpec((3, C, 128), lambda t, s: (0, 0, 0)),
         ],
         scratch_shapes=[
-            pltpu.VMEM((SPAN, 128), F32),
-            pltpu.VMEM((2, SPAN, 128), F32),
-            pltpu.VMEM((PLANE, 128), F32),
-            pltpu.VMEM((2, 3, PLANE, 128), F32),
-            pltpu.VMEM((PLANE, 128), F32),
-            pltpu.VMEM((2, 3, PLANE, 128), F32),
+            pltpu.VMEM((TOGETHER, SPAN, 128), F32),
+            pltpu.VMEM((2 * TOGETHER, SPAN, 128), F32),
+            pltpu.VMEM((TOGETHER, PLANE, 128), F32),
+            pltpu.VMEM((2 * TOGETHER, 3, PLANE, 128), F32),
+            pltpu.VMEM((TOGETHER, PLANE, 128), F32),
+            pltpu.VMEM((2 * TOGETHER, 3, PLANE, 128), F32),
             pltpu.VMEM((2, ROWS, 256), F32),
-            pltpu.VMEM((ROWS, 256), BF),
-            pltpu.VMEM((2, SLABS, ROWS, 128), BF),
-            pltpu.VMEM((PLANE, 128), F32),
-            pltpu.VMEM((3, PLANE, 128), F32),
+            pltpu.VMEM((TOGETHER, ROWS, 256), BF),
+            pltpu.VMEM((2 * TOGETHER, SLABS, ROWS, 128), BF),
+            pltpu.VMEM((TOGETHER, PLANE, 128), F32),
+            pltpu.VMEM((TOGETHER, 3, PLANE, 128), F32),
             pltpu.VMEM((256, 256), F32),
             pltpu.VMEM((2, tiles * TILE + 2 * STEP, 128), F32),
             pltpu.VMEM((2, tiles * TILE + 2 * STEP, 128), F32),

time: 95.8 us -> 93.8 us (0.979)
  Pallas kernels: 42.3 us -> 40.3 us
    pallas_call x1, Pallas kernels: 42.3 us -> 40.3 us  [run_tiles(): pl.pallas_call(functools.partial(tile_kernel, blocks, tiles), grid_spec=g...]
where the time goes in v5:
time: 93.8 us; the launch traced here: 93.5 us
  Pallas kernels  40.3 us (43%)
  blocking collectives  19.4 us (21%)
  waiting for transfers between devices  14.7 us (16%)
  starting transfers between devices  11.7 us (12%)
  local copies, waits for them, and re-layouts  3.77 us (4%)
  other arithmetic  1.78 us (2%)
  between operations  0.95 us (1%)
    pallas_call x1, Pallas kernels, run_tiles(): pl.pallas_call(functools.partial(tile_kernel, blocks, tiles), grid_spec=g...  40.3 us
    all_to_all x1, blocking collectives, per_device(): lax.all_to_all(terms.astype(BF), axes, 0, 0, axis_index_groups=same_core,...  19.4 us
    all_to_all x1, waiting for transfers between devices, per_device(): lax.all_to_all(jnp.broadcast_to(packed[None], (blocks, 32, 128)), axes, 0...  11.6 us
    all_to_all x1, starting transfers between devices, per_device(): lax.all_to_all(jnp.broadcast_to(packed[None], (blocks, 32, 128)), axes, 0...  11.5 us
    ppermute x1, waiting for transfers between devices, per_device(): other = lax.ppermute(sent, 'diag', swap)  1.92 us
  transfers between devices with their start and end apart: 3, of which 3 were waited for; matrix products, arithmetic and copies ran while one was open for 2% of the time, Pallas kernels for 0%

profile of v5, /device:TPU:0, one launch (start us, length us, event | category | flops | bytes accessed | tf_op | source)
XLA Modules:
  0.0 93.5 jit_solution(2205709777771769331)
XLA Ops:
  0.6 0.0 copy-start
  0.6 0.0 copy-start.2
  0.7 0.7 copy-done
  1.4 0.9 convolution_convert_fusion
  2.3 0.1 pad_maximum_fusion.5
  2.4 0.0 copy-start.6
  2.4 0.0 copy-start.3
  2.4 0.0 copy-start.4
  2.4 0.9 broadcast_in_dim.16
  3.2 11.5 %all-to-all-start = ((bf16[64,32,128]{2,1,0:T(8,128)(2,1)}), bf16[64,32,128]{2,1,0:T(8,128)(2,1)S(1)}, u32[]{:S(2)}, u32[]{:S(2)}) async-start(bf16[64,32,128]{2,1,0:T(8,128)(2,1)} %broadcast_in_dim.16), calls=%async_computation | async-start | bytes 1048576 | tf_op jit(solution)/shard_map/all_to_all | solution.py:644
  14.8 0.0 copy-done.2
  14.8 0.1 copy.26
  14.9 0.0 copy-start.5
  15.0 0.0 copy-done.6
  15.0 0.1 select_reduce_fusion
  15.1 0.0 copy-done.3
  15.1 0.1 stack_tile.6
  15.2 0.0 copy-done.4
  15.2 0.1 stack_tile.7
  15.4 0.1 bitcast_dynamic-update-slice_fusion.5
  15.4 0.1 bitcast_dynamic-update-slice_fusion.4
  15.5 0.1 bitcast_dynamic-update-slice_fusion.2
  15.6 0.1 bitcast_dynamic-update-slice_fusion
  15.8 0.1 compare_convert_fusion
  15.9 0.1 fusion.17
  16.0 11.6 %all-to-all-done.mine_ref = bf16[64,32,128]{2,1,0:T(8,128)(2,1)S(1)} async-done(((bf16[64,32,128]{2,1,0:T(8,128)(2,1)}), bf16[64,32,128]{2,1,0:T(8,128)(2,1)S(1)}, u32[]{:S(2)}, u32[]{:S(2)}) %all-to-all-start) | async-done | bytes 524320 | tf_op jit(solution)/shard_map/all_to_all | solution.py:644
  27.6 0.0 collective-permute-start
  27.6 0.0 copy-done.5
  27.6 0.1 pad_add_fusion.s_ref
  27.7 0.4 reshape.309
  28.0 0.1 copy.18.wf_ref
  28.2 0.0 copy-start.1
  28.2 0.1 pad_maximum_fusion.1.place_ref
  28.3 0.1 fusion.2.pick_ref
  28.4 1.1 %collective-permute-done.theirs_ref = bf16[64,32,128]{2,1,0:T(8,128)(2,1)S(1)} collective-permute-done((bf16[64,32,128]{2,1,0:T(8,128)(2,1)S(1)}, bf16[64,32,128]{2,1,0:T(8,128)(2,1)S(1)}, u32[]{:S(2)}, u32[]{:S(2)}) %collective-permute-start) | collective-permute-done | bytes 524320 | tf_op jit(solution)/shard_map/ppermute | solution.py:652
  29.5 0.0 copy-done.1
  29.5 40.3 %shard_map.95 = (f32[64,32,128]{2,1,0:T(8,128)S(1)}, bf16[64,32,128]{2,1,0:T(8,128)(2,1)S(1)}, f32[3,32,128]{2,1,0:T(8,128)S(1)}) custom-call(s32[130]{0:T(256)S(1)} %pad_add_fusion.s_ref, bf16[64,32,128]{2,1,0:T(8,128)(2,1)S(1)} %all-to-all-done.mine_ref, bf16[64,32,128]{2,1,0:T(8,128)(2,1)S(1)} %collective-permute-done.theirs_ref, ...), custom_call_target="tpu_custom_call" | custom-call | tf_op jit(solution)/shard_map/pallas_call | solution.py:600
  69.8 0.1 div.102
  70.0 0.1 div.104
  70.1 0.1 pad_bitcast_fusion
  70.1 0.1 copy.24
  70.3 0.1 pad_maximum_fusion
  70.3 0.2 collective-permute-start.1
  70.6 1.9 %collective-permute-done.1 = bf16[64,40,128]{2,1,0:T(8,128)(2,1)S(1)} collective-permute-done((bf16[64,40,128]{2,1,0:T(8,128)(2,1)S(1)}, bf16[64,40,128]{2,1,0:T(8,128)(2,1)S(1)}, u32[]{:S(2)}, u32[]{:S(2)}) %collective-permute-start.1) | collective-permute-done | bytes 655392 | tf_op jit(solution)/shard_map/ppermute | solution.py:689
  72.5 0.2 fusion
  72.7 19.4 %all_to_all.10 = bf16[64,40,128]{2,1,0:T(8,128)(2,1)S(1)} all-to-all(bf16[64,40,128]{2,1,0:T(8,128)(2,1)S(1)} %fusion), channel_id=1, replica_groups={{0,2,4,6,8,10,12,14,16,18,20,22,24,26,28,30,32,34,36,38,40,42,44,46,48,..., dimensions={0} | all-to-all | bytes 1310720 | tf_op jit(solution)/shard_map/all_to_all | solution.py:691
  92.1 0.1 convert_reduce_fusion
  92.3 0.5 slice_bitcast_fusion.2
  92.8 0.1 fusion.42
  92.8 0.6 pad_maximum_fusion.4
  (23 shorter events, 0.5 us)
Async XLA Ops:
  0.6 0.8 copy-start
  0.6 14.2 %copy-start.2 = (bf16[9,32,32]{2,1,0:T(8,128)(2,1)S(1)}, bf16[9,32,32]{2,1,0:T(8,128)(2,1)}, u32[]{:S(2)}) copy-start(bf16[9,32,32]{2,1,0:T(8,128)(2,1)} %param.10) | copy-start | bytes 55300
  2.4 12.6 %copy-start.6 = (s32[64]{0:T(128)S(1)}, s32[64]{0:T(128)}, u32[]{:S(2)}) copy-start(s32[64]{0:T(128)} %param.14) | copy-start | bytes 772
  2.4 12.7 %copy-start.3 = (f32[32]{0:T(128)S(1)}, f32[32]{0:T(128)}, u32[]{:S(2)}) copy-start(f32[32]{0:T(128)} %param.11) | copy-start | bytes 388
  2.4 12.8 %copy-start.4 = (f32[32]{0:T(128)S(1)}, f32[32]{0:T(128)}, u32[]{:S(2)}) copy-start(f32[32]{0:T(128)} %param.12) | copy-start | bytes 388
  3.2 24.4 %all-to-all-start = ((bf16[64,32,128]{2,1,0:T(8,128)(2,1)}), bf16[64,32,128]{2,1,0:T(8,128)(2,1)S(1)}, u32[]{:S(2)}, u32[]{:S(2)}) async-start(bf16[64,32,128]{2,1,0:T(8,128)(2,1)} %broadcast_in_dim.16), calls=%async_computation | async-start | bytes 1048576 | tf_op jit(solution)/shard_map/all_to_all | solution.py:644
  14.9 12.7 %copy-start.5 = (s32[64]{0:T(128)S(1)}, s32[64]{0:T(128)}, u32[]{:S(2)}) copy-start(s32[64]{0:T(128)} %param.15) | copy-start | bytes 772
  27.6 1.9 %collective-permute-start = (bf16[64,32,128]{2,1,0:T(8,128)(2,1)S(1)}, bf16[64,32,128]{2,1,0:T(8,128)(2,1)S(1)}, u32[]{:S(2)}, u32[]{:S(2)}) collective-permute-start(bf16[64,32,128]{2,1,0:T(8,128)(2,1)S(1)} %all-to-all-done.mine_ref), channel_id=1, source_target_pairs={{0,1},{1,0},{2,3},{3,2},{4,5},{5,4},{6,7},{7,6},{8,9},{9,8},{10,11... | collective-permute-start | bytes 1572872 | tf_op jit(solution)/shard_map/ppermute | solution.py:652
  28.2 1.4 %copy-start.1 = (bf16[8,128,128]{2,1,0:T(8,128)(2,1)S(1)}, bf16[8,128,128]{2,1,0:T(8,128)(2,1)}, u32[]{:S(2)}) copy-start(bf16[8,128,128]{2,1,0:T(8,128)(2,1)} %tgt_ref.1) | copy-start | bytes 786436
  70.3 2.2 %collective-permute-start.1 = (bf16[64,40,128]{2,1,0:T(8,128)(2,1)S(1)}, bf16[64,40,128]{2,1,0:T(8,128)(2,1)S(1)}, u32[]{:S(2)}, u32[]{:S(2)}) collective-permute-start(bf16[64,40,128]{2,1,0:T(8,128)(2,1)S(1)} %pad_maximum_fusion), channel_id=1, source_target_pairs={{0,1},{1,0},{2,3},{3,2},{4,5},{5,4},{6,7},{7,6},{8,9},{9,8},{10,11... | collective-permute-start | bytes 1966088 | tf_op jit(solution)/shard_map/ppermute | solution.py:689

commit v6 on v5

--- a/solution.py
+++ b/solution.py
@@ -46,11 +46,6 @@
     ]
     p, q = x
     return jnp.where(odd, p + pltpu.roll(p, 1, 0), q + pltpu.roll(q, 7, 0))
-
-
-def lane_fold(x):
-    x = x + pltpu.roll(x, 64, 1)
-    return x + pltpu.roll(x, 32, 1)
 
 
 def weave(*streams):
@@ -481,8 +476,11 @@
         low_half = lax.broadcasted_iota(jnp.int32, (32, 128), 1) < 64
         even = lax.broadcasted_iota(jnp.int32, row_acc.shape[1:], 1) // C % 2 == 0
         for acc_ref in (row_acc, col_acc):
-            acc_ref[0] = jnp.where(even, lane_fold(acc_ref[0]), lane_fold(acc_ref[1]))
-
+            plain, scaled = acc_ref[0], acc_ref[1]
+            sums = jnp.where(even, plain, scaled) + pltpu.roll(
+                jnp.where(even, scaled, plain), 32, 1
+            )
+            acc_ref[0] = sums + pltpu.roll(sums, 64, 1)
 
         def put(acc_ref, base, k, begin, count):
             n = base + k

time: 93.8 us -> 93.2 us (level)
  no operation moved by 1% of the time
where the time goes in v6:
time: 93.2 us; the launch traced here: 92.9 us
  Pallas kernels  39.7 us (43%)
  blocking collectives  19.4 us (21%)
  waiting for transfers between devices  14.7 us (16%)
  starting transfers between devices  11.7 us (13%)
  local copies, waits for them, and re-layouts  3.77 us (4%)
  other arithmetic  1.78 us (2%)
  between operations  0.95 us (1%)
    pallas_call x1, Pallas kernels, run_tiles(): pl.pallas_call(functools.partial(tile_kernel, blocks, tiles), grid_spec=g...  39.7 us
    all_to_all x1, blocking collectives, per_device(): lax.all_to_all(terms.astype(BF), axes, 0, 0, axis_index_groups=same_core,...  19.4 us
    all_to_all x1, waiting for transfers between devices, per_device(): lax.all_to_all(jnp.broadcast_to(packed[None], (blocks, 32, 128)), axes, 0...  11.6 us
    all_to_all x1, starting transfers between devices, per_device(): lax.all_to_all(jnp.broadcast_to(packed[None], (blocks, 32, 128)), axes, 0...  11.5 us
    ppermute x1, waiting for transfers between devices, per_device(): other = lax.ppermute(sent, 'diag', swap)  1.92 us
  transfers between devices with their start and end apart: 3, of which 3 were waited for; matrix products, arithmetic and copies ran while one was open for 2% of the time, Pallas kernels for 0%

profile of v6, /device:TPU:0, one launch (start us, length us, event | category | flops | bytes accessed | tf_op | source)
XLA Modules:
  0.0 92.9 jit_solution(8535382460484512340)
XLA Ops:
  0.6 0.0 copy-start
  0.6 0.0 copy-start.2
  0.7 0.7 copy-done
  1.4 0.9 convolution_convert_fusion
  2.3 0.1 pad_maximum_fusion.5
  2.4 0.0 copy-start.6
  2.4 0.0 copy-start.3
  2.4 0.0 copy-start.4
  2.4 0.9 broadcast_in_dim.16
  3.2 11.5 %all-to-all-start = ((bf16[64,32,128]{2,1,0:T(8,128)(2,1)}), bf16[64,32,128]{2,1,0:T(8,128)(2,1)S(1)}, u32[]{:S(2)}, u32[]{:S(2)}) async-start(bf16[64,32,128]{2,1,0:T(8,128)(2,1)} %broadcast_in_dim.16), calls=%async_computation | async-start | bytes 1048576 | tf_op jit(solution)/shard_map/all_to_all | solution.py:642
  14.8 0.0 copy-done.2
  14.8 0.1 copy.26
  14.9 0.0 copy-start.5
  15.0 0.0 copy-done.6
  15.0 0.1 select_reduce_fusion
  15.1 0.0 copy-done.3
  15.1 0.1 stack_tile.6
  15.2 0.0 copy-done.4
  15.2 0.1 stack_tile.7
  15.4 0.1 bitcast_dynamic-update-slice_fusion.5
  15.4 0.1 bitcast_dynamic-update-slice_fusion.4
  15.5 0.1 bitcast_dynamic-update-slice_fusion.2
  15.6 0.1 bitcast_dynamic-update-slice_fusion
  15.8 0.1 compare_convert_fusion
  15.9 0.1 fusion.17
  16.0 11.6 %all-to-all-done.mine_ref = bf16[64,32,128]{2,1,0:T(8,128)(2,1)S(1)} async-done(((bf16[64,32,128]{2,1,0:T(8,128)(2,1)}), bf16[64,32,128]{2,1,0:T(8,128)(2,1)S(1)}, u32[]{:S(2)}, u32[]{:S(2)}) %all-to-all-start) | async-done | bytes 524320 | tf_op jit(solution)/shard_map/all_to_all | solution.py:642
  27.6 0.0 collective-permute-start
  27.6 0.0 copy-done.5
  27.6 0.1 pad_add_fusion.s_ref
  27.7 0.4 reshape.309
  28.0 0.1 copy.18.wf_ref
  28.2 0.0 copy-start.1
  28.2 0.1 pad_maximum_fusion.1.place_ref
  28.3 0.1 fusion.2.pick_ref
  28.4 1.1 %collective-permute-done.theirs_ref = bf16[64,32,128]{2,1,0:T(8,128)(2,1)S(1)} collective-permute-done((bf16[64,32,128]{2,1,0:T(8,128)(2,1)S(1)}, bf16[64,32,128]{2,1,0:T(8,128)(2,1)S(1)}, u32[]{:S(2)}, u32[]{:S(2)}) %collective-permute-start) | collective-permute-done | bytes 524320 | tf_op jit(solution)/shard_map/ppermute | solution.py:650
  29.5 0.0 copy-done.1
  29.5 39.7 %shard_map.95 = (f32[64,32,128]{2,1,0:T(8,128)S(1)}, bf16[64,32,128]{2,1,0:T(8,128)(2,1)S(1)}, f32[3,32,128]{2,1,0:T(8,128)S(1)}) custom-call(s32[130]{0:T(256)S(1)} %pad_add_fusion.s_ref, bf16[64,32,128]{2,1,0:T(8,128)(2,1)S(1)} %all-to-all-done.mine_ref, bf16[64,32,128]{2,1,0:T(8,128)(2,1)S(1)} %collective-permute-done.theirs_ref, ...), custom_call_target="tpu_custom_call" | custom-call | tf_op jit(solution)/shard_map/pallas_call | solution.py:598
  69.3 0.1 div.102
  69.4 0.1 div.104
  69.5 0.1 pad_bitcast_fusion
  69.6 0.1 copy.24
  69.7 0.1 pad_maximum_fusion
  69.8 0.2 collective-permute-start.1
  70.0 1.9 %collective-permute-done.1 = bf16[64,40,128]{2,1,0:T(8,128)(2,1)S(1)} collective-permute-done((bf16[64,40,128]{2,1,0:T(8,128)(2,1)S(1)}, bf16[64,40,128]{2,1,0:T(8,128)(2,1)S(1)}, u32[]{:S(2)}, u32[]{:S(2)}) %collective-permute-start.1) | collective-permute-done | bytes 655392 | tf_op jit(solution)/shard_map/ppermute | solution.py:687
  72.0 0.2 fusion
  72.2 19.4 %all_to_all.10 = bf16[64,40,128]{2,1,0:T(8,128)(2,1)S(1)} all-to-all(bf16[64,40,128]{2,1,0:T(8,128)(2,1)S(1)} %fusion), channel_id=1, replica_groups={{0,2,4,6,8,10,12,14,16,18,20,22,24,26,28,30,32,34,36,38,40,42,44,46,48,..., dimensions={0} | all-to-all | bytes 1310720 | tf_op jit(solution)/shard_map/all_to_all | solution.py:689
  91.6 0.1 convert_reduce_fusion
  91.7 0.5 slice_bitcast_fusion.2
  92.2 0.1 fusion.42
  92.3 0.6 pad_maximum_fusion.4
  (23 shorter events, 0.5 us)
Async XLA Ops:
  0.6 0.8 copy-start
  0.6 14.2 %copy-start.2 = (bf16[9,32,32]{2,1,0:T(8,128)(2,1)S(1)}, bf16[9,32,32]{2,1,0:T(8,128)(2,1)}, u32[]{:S(2)}) copy-start(bf16[9,32,32]{2,1,0:T(8,128)(2,1)} %param.10) | copy-start | bytes 55300
  2.4 12.6 %copy-start.6 = (s32[64]{0:T(128)S(1)}, s32[64]{0:T(128)}, u32[]{:S(2)}) copy-start(s32[64]{0:T(128)} %param.14) | copy-start | bytes 772
  2.4 12.7 %copy-start.3 = (f32[32]{0:T(128)S(1)}, f32[32]{0:T(128)}, u32[]{:S(2)}) copy-start(f32[32]{0:T(128)} %param.11) | copy-start | bytes 388
  2.4 12.8 %copy-start.4 = (f32[32]{0:T(128)S(1)}, f32[32]{0:T(128)}, u32[]{:S(2)}) copy-start(f32[32]{0:T(128)} %param.12) | copy-start | bytes 388
  3.2 24.4 %all-to-all-start = ((bf16[64,32,128]{2,1,0:T(8,128)(2,1)}), bf16[64,32,128]{2,1,0:T(8,128)(2,1)S(1)}, u32[]{:S(2)}, u32[]{:S(2)}) async-start(bf16[64,32,128]{2,1,0:T(8,128)(2,1)} %broadcast_in_dim.16), calls=%async_computation | async-start | bytes 1048576 | tf_op jit(solution)/shard_map/all_to_all | solution.py:642
  14.9 12.7 %copy-start.5 = (s32[64]{0:T(128)S(1)}, s32[64]{0:T(128)}, u32[]{:S(2)}) copy-start(s32[64]{0:T(128)} %param.15) | copy-start | bytes 772
  27.6 1.9 %collective-permute-start = (bf16[64,32,128]{2,1,0:T(8,128)(2,1)S(1)}, bf16[64,32,128]{2,1,0:T(8,128)(2,1)S(1)}, u32[]{:S(2)}, u32[]{:S(2)}) collective-permute-start(bf16[64,32,128]{2,1,0:T(8,128)(2,1)S(1)} %all-to-all-done.mine_ref), channel_id=1, source_target_pairs={{0,1},{1,0},{2,3},{3,2},{4,5},{5,4},{6,7},{7,6},{8,9},{9,8},{10,11... | collective-permute-start | bytes 1572872 | tf_op jit(solution)/shard_map/ppermute | solution.py:650
  28.2 1.4 %copy-start.1 = (bf16[8,128,128]{2,1,0:T(8,128)(2,1)S(1)}, bf16[8,128,128]{2,1,0:T(8,128)(2,1)}, u32[]{:S(2)}) copy-start(bf16[8,128,128]{2,1,0:T(8,128)(2,1)} %tgt_ref.1) | copy-start | bytes 786436
  69.8 2.2 %collective-permute-start.1 = (bf16[64,40,128]{2,1,0:T(8,128)(2,1)S(1)}, bf16[64,40,128]{2,1,0:T(8,128)(2,1)S(1)}, u32[]{:S(2)}, u32[]{:S(2)}) collective-permute-start(bf16[64,40,128]{2,1,0:T(8,128)(2,1)S(1)} %pad_maximum_fusion), channel_id=1, source_target_pairs={{0,1},{1,0},{2,3},{3,2},{4,5},{5,4},{6,7},{7,6},{8,9},{9,8},{10,11... | collective-permute-start | bytes 1966088 | tf_op jit(solution)/shard_map/ppermute | solution.py:687

commit v7 on v6

--- a/solution.py
+++ b/solution.py
@@ -100,16 +100,19 @@
         acc_s[...] = jnp.zeros_like(acc_s)
         row_acc[...] = jnp.zeros_like(row_acc)
         col_acc[...] = jnp.zeros_like(col_acc)
-        line = lax.broadcasted_iota(jnp.int32, (ROWS, 256), 0)
-        lane = lax.broadcasted_iota(jnp.int32, (ROWS, 256), 1)
-        r = line // PLANE
-        jp = (line % PLANE) // STEP
+        line = lax.broadcasted_iota(jnp.int32, (PLANE, 256), 0)
+        lane = lax.broadcasted_iota(jnp.int32, (PLANE, 256), 1)
+        jp = line // STEP
         s = line % STEP
         ii = lane // 64
         jj = (lane // 32) % 2
+        plane = (TILE * d + 32 * jp + s + 16 * (jj - ii)).astype(F32)
         for ig in range(2):
-            dist = TILE * d - 64 * ig + 32 * jp + s - r + 16 * (jj - ii)
-            dist_s[ig] = jnp.where(dist >= 0, dist, 1 << 20).astype(F32)
+            for r in range(STEP):
+                dist = plane - (64 * ig + r)
+                dist_s[ig, r * PLANE : (r + 1) * PLANE, :] = jnp.where(
+                    dist >= 0, dist, 1048576.0
+                )
 
     core = s_ref[2 * blocks + 1] % 2
 

time: 93.2 us -> 92.9 us (level)
  no operation moved by 1% of the time
where the time goes in v7:
time: 92.9 us; the launch traced here: 92.6 us
  Pallas kernels  39.4 us (42%)
  blocking collectives  19.4 us (21%)
  waiting for transfers between devices  14.7 us (16%)
  starting transfers between devices  11.7 us (13%)
  local copies, waits for them, and re-layouts  3.77 us (4%)
  other arithmetic  1.78 us (2%)
  between operations  0.95 us (1%)
    pallas_call x1, Pallas kernels, run_tiles(): pl.pallas_call(functools.partial(tile_kernel, blocks, tiles), grid_spec=g...  39.4 us
    all_to_all x1, blocking collectives, per_device(): lax.all_to_all(terms.astype(BF), axes, 0, 0, axis_index_groups=same_core,...  19.4 us
    all_to_all x1, waiting for transfers between devices, per_device(): lax.all_to_all(jnp.broadcast_to(packed[None], (blocks, 32, 128)), axes, 0...  11.6 us
    all_to_all x1, starting transfers between devices, per_device(): lax.all_to_all(jnp.broadcast_to(packed[None], (blocks, 32, 128)), axes, 0...  11.5 us
    ppermute x1, waiting for transfers between devices, per_device(): other = lax.ppermute(sent, 'diag', swap)  1.92 us
  transfers between devices with their start and end apart: 3, of which 3 were waited for; matrix products, arithmetic and copies ran while one was open for 2% of the time, Pallas kernels for 0%

profile of v7, /device:TPU:0, one launch (start us, length us, event | category | flops | bytes accessed | tf_op | source)
XLA Modules:
  0.0 92.6 jit_solution(6505317692726593787)
XLA Ops:
  0.6 0.0 copy-start
  0.6 0.0 copy-start.2
  0.7 0.7 copy-done
  1.4 0.9 convolution_convert_fusion
  2.3 0.1 pad_maximum_fusion.5
  2.4 0.0 copy-start.6
  2.4 0.0 copy-start.3
  2.4 0.0 copy-start.4
  2.4 0.9 broadcast_in_dim.16
  3.2 11.5 %all-to-all-start = ((bf16[64,32,128]{2,1,0:T(8,128)(2,1)}), bf16[64,32,128]{2,1,0:T(8,128)(2,1)S(1)}, u32[]{:S(2)}, u32[]{:S(2)}) async-start(bf16[64,32,128]{2,1,0:T(8,128)(2,1)} %broadcast_in_dim.16), calls=%async_computation | async-start | bytes 1048576 | tf_op jit(solution)/shard_map/all_to_all | solution.py:645
  14.8 0.0 copy-done.2
  14.8 0.1 copy.26
  14.9 0.0 copy-start.5
  15.0 0.0 copy-done.6
  15.0 0.1 select_reduce_fusion
  15.1 0.0 copy-done.3
  15.1 0.1 stack_tile.6
  15.2 0.0 copy-done.4
  15.2 0.1 stack_tile.7
  15.4 0.1 bitcast_dynamic-update-slice_fusion.5
  15.4 0.1 bitcast_dynamic-update-slice_fusion.4
  15.5 0.1 bitcast_dynamic-update-slice_fusion.2
  15.6 0.1 bitcast_dynamic-update-slice_fusion
  15.8 0.1 compare_convert_fusion
  15.9 0.1 fusion.17
  16.0 11.6 %all-to-all-done.mine_ref = bf16[64,32,128]{2,1,0:T(8,128)(2,1)S(1)} async-done(((bf16[64,32,128]{2,1,0:T(8,128)(2,1)}), bf16[64,32,128]{2,1,0:T(8,128)(2,1)S(1)}, u32[]{:S(2)}, u32[]{:S(2)}) %all-to-all-start) | async-done | bytes 524320 | tf_op jit(solution)/shard_map/all_to_all | solution.py:645
  27.6 0.0 collective-permute-start
  27.6 0.0 copy-done.5
  27.6 0.1 pad_add_fusion.s_ref
  27.7 0.4 reshape.309
  28.0 0.1 copy.18.wf_ref
  28.2 0.0 copy-start.1
  28.2 0.1 pad_maximum_fusion.1.place_ref
  28.3 0.1 fusion.2.pick_ref
  28.4 1.1 %collective-permute-done.theirs_ref = bf16[64,32,128]{2,1,0:T(8,128)(2,1)S(1)} collective-permute-done((bf16[64,32,128]{2,1,0:T(8,128)(2,1)S(1)}, bf16[64,32,128]{2,1,0:T(8,128)(2,1)S(1)}, u32[]{:S(2)}, u32[]{:S(2)}) %collective-permute-start) | collective-permute-done | bytes 524320 | tf_op jit(solution)/shard_map/ppermute | solution.py:653
  29.5 0.0 copy-done.1
  29.5 39.4 %shard_map.95 = (f32[64,32,128]{2,1,0:T(8,128)S(1)}, bf16[64,32,128]{2,1,0:T(8,128)(2,1)S(1)}, f32[3,32,128]{2,1,0:T(8,128)S(1)}) custom-call(s32[130]{0:T(256)S(1)} %pad_add_fusion.s_ref, bf16[64,32,128]{2,1,0:T(8,128)(2,1)S(1)} %all-to-all-done.mine_ref, bf16[64,32,128]{2,1,0:T(8,128)(2,1)S(1)} %collective-permute-done.theirs_ref, ...), custom_call_target="tpu_custom_call" | custom-call | tf_op jit(solution)/shard_map/pallas_call | solution.py:601
  68.9 0.1 div.102
  69.1 0.1 div.104
  69.2 0.1 pad_bitcast_fusion
  69.3 0.1 copy.24
  69.4 0.1 pad_maximum_fusion
  69.5 0.2 collective-permute-start.1
  69.7 1.9 %collective-permute-done.1 = bf16[64,40,128]{2,1,0:T(8,128)(2,1)S(1)} collective-permute-done((bf16[64,40,128]{2,1,0:T(8,128)(2,1)S(1)}, bf16[64,40,128]{2,1,0:T(8,128)(2,1)S(1)}, u32[]{:S(2)}, u32[]{:S(2)}) %collective-permute-start.1) | collective-permute-done | bytes 655392 | tf_op jit(solution)/shard_map/ppermute | solution.py:690
  71.7 0.2 fusion
  71.8 19.4 %all_to_all.10 = bf16[64,40,128]{2,1,0:T(8,128)(2,1)S(1)} all-to-all(bf16[64,40,128]{2,1,0:T(8,128)(2,1)S(1)} %fusion), channel_id=1, replica_groups={{0,2,4,6,8,10,12,14,16,18,20,22,24,26,28,30,32,34,36,38,40,42,44,46,48,..., dimensions={0} | all-to-all | bytes 1310720 | tf_op jit(solution)/shard_map/all_to_all | solution.py:692
  91.3 0.1 convert_reduce_fusion
  91.4 0.5 slice_bitcast_fusion.2
  91.9 0.1 fusion.42
  92.0 0.6 pad_maximum_fusion.4
  (23 shorter events, 0.5 us)
Async XLA Ops:
  0.6 0.8 copy-start
  0.6 14.2 %copy-start.2 = (bf16[9,32,32]{2,1,0:T(8,128)(2,1)S(1)}, bf16[9,32,32]{2,1,0:T(8,128)(2,1)}, u32[]{:S(2)}) copy-start(bf16[9,32,32]{2,1,0:T(8,128)(2,1)} %param.10) | copy-start | bytes 55300
  2.4 12.6 %copy-start.6 = (s32[64]{0:T(128)S(1)}, s32[64]{0:T(128)}, u32[]{:S(2)}) copy-start(s32[64]{0:T(128)} %param.14) | copy-start | bytes 772
  2.4 12.7 %copy-start.3 = (f32[32]{0:T(128)S(1)}, f32[32]{0:T(128)}, u32[]{:S(2)}) copy-start(f32[32]{0:T(128)} %param.11) | copy-start | bytes 388
  2.4 12.8 %copy-start.4 = (f32[32]{0:T(128)S(1)}, f32[32]{0:T(128)}, u32[]{:S(2)}) copy-start(f32[32]{0:T(128)} %param.12) | copy-start | bytes 388
  3.2 24.4 %all-to-all-start = ((bf16[64,32,128]{2,1,0:T(8,128)(2,1)}), bf16[64,32,128]{2,1,0:T(8,128)(2,1)S(1)}, u32[]{:S(2)}, u32[]{:S(2)}) async-start(bf16[64,32,128]{2,1,0:T(8,128)(2,1)} %broadcast_in_dim.16), calls=%async_computation | async-start | bytes 1048576 | tf_op jit(solution)/shard_map/all_to_all | solution.py:645
  14.9 12.7 %copy-start.5 = (s32[64]{0:T(128)S(1)}, s32[64]{0:T(128)}, u32[]{:S(2)}) copy-start(s32[64]{0:T(128)} %param.15) | copy-start | bytes 772
  27.6 1.9 %collective-permute-start = (bf16[64,32,128]{2,1,0:T(8,128)(2,1)S(1)}, bf16[64,32,128]{2,1,0:T(8,128)(2,1)S(1)}, u32[]{:S(2)}, u32[]{:S(2)}) collective-permute-start(bf16[64,32,128]{2,1,0:T(8,128)(2,1)S(1)} %all-to-all-done.mine_ref), channel_id=1, source_target_pairs={{0,1},{1,0},{2,3},{3,2},{4,5},{5,4},{6,7},{7,6},{8,9},{9,8},{10,11... | collective-permute-start | bytes 1572872 | tf_op jit(solution)/shard_map/ppermute | solution.py:653
  28.2 1.4 %copy-start.1 = (bf16[8,128,128]{2,1,0:T(8,128)(2,1)S(1)}, bf16[8,128,128]{2,1,0:T(8,128)(2,1)}, u32[]{:S(2)}) copy-start(bf16[8,128,128]{2,1,0:T(8,128)(2,1)} %tgt_ref.1) | copy-start | bytes 786436
  69.5 2.2 %collective-permute-start.1 = (bf16[64,40,128]{2,1,0:T(8,128)(2,1)S(1)}, bf16[64,40,128]{2,1,0:T(8,128)(2,1)S(1)}, u32[]{:S(2)}, u32[]{:S(2)}) collective-permute-start(bf16[64,40,128]{2,1,0:T(8,128)(2,1)S(1)} %pad_maximum_fusion), channel_id=1, source_target_pairs={{0,1},{1,0},{2,3},{3,2},{4,5},{5,4},{6,7},{7,6},{8,9},{9,8},{10,11... | collective-permute-start | bytes 1966088 | tf_op jit(solution)/shard_map/ppermute | solution.py:690
